TPU v7x, 256 devices: a whole 4x4x8 slice. The times are simulated.
256 devices in a mesh: dom: 128 (over x, z, y), col: 2 (over core).
Axes of the slice: x: 4, y: 4, z: 8, core: 2. Of those that a mesh axis runs over, the one named last changes fastest.
Arguments:
- first_interp: bfloat16 [8192, 4, 128, 128], P('dom'), may hold values from -0.25 to 0.25
- first_ids: int32 [8192, 4], P('dom'), may hold values from 0 to 7
- second_interp: bfloat16 [1024, 128, 1024], P('dom', None, 'col'), may hold values from -6 to 6
- coupling: bfloat16 [4096, 128, 128], P('dom'), may hold values from -0.25 to 0.25
- send_rows: int32 [512, 8], P('dom'), may hold values from 0 to 7, each once within a row
- targets: int32 [1024], P('dom'), may hold values from 0 to 63
- keep_mask: int32 [8192, 8], P('dom', 'col'), may hold values from 0 to 1, as said below
Outputs:
- interp: bfloat16 [8192, 128, 1024], P('dom', None, 'col')
Inputs may be any that keep to these rules, and one draw needn't show every extreme that they name: `keep_mask`: every fine row block keeps at least one block of columns.
All inputs are finite; a program needn't handle non-finite values.
Results may differ from a plain program's by a relative error of at most 0.001.
Values may be sent and summed in bfloat16 or wider, within the bound.
No kernel may reach another device: no remote copies, remote signals or barrier semaphores. Data moves between devices by JAX's collectives and lax.ppermute only.
A program may use at most 192 MiB of HBM per device.

v0:
```python
import jax
import jax.numpy as jnp
from jax import lax
from jax.sharding import PartitionSpec as P

G = 4


epsilon = 1e-06


def partner(block, axis, distance):
    count = lax.axis_size(axis)
    route = []
    for low in range(count):
        high = low | 1 << distance
        if high != low and high < count:
            route += [(low, high), (high, low)]
    return lax.ppermute(block, axis, route)


def on_device(first_interp, first_ids, second_interp, coupling, send_rows, targets, keep_mask):
    fine_count = first_ids.shape[0]
    mid_count = second_interp.shape[0]
    block_size = second_interp.shape[1]
    half_width = second_interp.shape[2]
    level_count = send_rows.shape[0]
    group_count = targets.shape[0] // level_count
    tiles = coupling.reshape(level_count, mid_count, block_size, block_size)
    target_table = targets.reshape(level_count, group_count)
    gathered = second_interp[first_ids]
    raw = jnp.einsum("fkab,fkbn->fan", first_interp, gathered, preferred_element_type=jnp.float32)
    grouped_all = []
    for interface_bit_level in range(level_count):
        own_rows = second_interp[send_rows[interface_bit_level]]
        incoming = partner(own_rows, "dom", interface_bit_level)
        products = jnp.einsum(
            "sab,sbn->san", tiles[interface_bit_level], incoming, preferred_element_type=jnp.float32
        )
        grouped = jnp.sum(products.reshape(group_count, G, block_size, half_width), axis=1)
        grouped_all.append(grouped)
    for bit_level in range(level_count):
        raw = raw.at[target_table[bit_level]].add(grouped_all[bit_level])
    column_blocks = keep_mask.shape[1]
    magnitude = jnp.abs(raw)
    weights = keep_mask.astype(jnp.float32)[:, None, :, None]
    full_part = jnp.sum(magnitude, axis=2)
    kept_part = jnp.sum(
        magnitude.reshape(fine_count, block_size, column_blocks, block_size) * weights, axis=(2, 3)
    )
    full, kept = lax.psum((full_part, kept_part), "col")
    scale = full / (kept + epsilon)
    kept_raw = (raw.reshape(fine_count, block_size, column_blocks, block_size) * weights).reshape(
        fine_count, block_size, half_width
    )
    return (kept_raw * scale[:, :, None]).astype(jnp.bfloat16)


def solution(mesh):
    return jax.shard_map(
        on_device,
        mesh=mesh,
        in_specs=(
            P("dom", None, None, None),
            P("dom", None),
            P("dom", None, "col"),
            P("dom", None, None),
            P("dom", None),
            P("dom"),
            P("dom", "col"),
        ),
        out_specs=P("dom", None, "col"),
        check_vma=False,
    )
```

profile of v0, /device:TPU:1, one launch (start us, length us, event | category | flops | bytes accessed | tf_op | source)
XLA Modules:
  0.0 151.0 jit_solution(5191787311926293472)
XLA Ops:
  6.5 0.0 copy-start
  6.5 0.0 copy-start.3
  6.5 0.0 all-reduce.3.cloned.1.call-start
  6.5 0.8 fusion.19
  7.4 0.4 copy-done
  7.8 0.6 gather_fusion.1
  8.4 0.7 copy.21
  9.1 2.2 %collective-permute-start = (bf16[8,128,512]{1,2,0:T(8,128)(2,1)S(1)}, bf16[8,128,512]{1,2,0:T(8,128)(2,1)}, u32[]{:S(2)}, u32[]{:S(2)}) collective-permute-start(bf16[8,128,512]{1,2,0:T(8,128)(2,1)S(1)} %copy.21), channel_id=1, source_target_pairs={{0,2},{2,0},{4,6},{6,4},{8,10},{10,8},{12,14},{14,12},{16,18},{18,... | collective-permute-start | bytes 3145736 | tf_op jit(solution)/shard_map/ppermute | solution.py:19
  11.3 0.6 gather_fusion.2
  11.9 1.3 copy.24
  13.3 2.6 %collective-permute-start.1 = (bf16[8,128,512]{1,2,0:T(8,128)(2,1)}, bf16[8,128,512]{1,2,0:T(8,128)(2,1)}, u32[]{:S(2)}, u32[]{:S(2)}) collective-permute-start(bf16[8,128,512]{1,2,0:T(8,128)(2,1)} %copy.24), channel_id=1, source_target_pairs={{0,4},{4,0},{2,6},{6,2},{8,12},{12,8},{10,14},{14,10},{16,20},{20,... | collective-permute-start | bytes 3145736 | tf_op jit(solution)/shard_map/ppermute | solution.py:19
  15.9 0.6 gather_fusion.3
  16.5 1.3 copy.26
  17.8 1.6 %collective-permute-start.2 = (bf16[8,128,512]{1,2,0:T(8,128)(2,1)}, bf16[8,128,512]{1,2,0:T(8,128)(2,1)}, u32[]{:S(2)}, u32[]{:S(2)}) collective-permute-start(bf16[8,128,512]{1,2,0:T(8,128)(2,1)} %copy.26), channel_id=1, source_target_pairs={{0,8},{8,0},{2,10},{10,2},{4,12},{12,4},{6,14},{14,6},{16,24},{24,... | collective-permute-start | bytes 3145736 | tf_op jit(solution)/shard_map/ppermute | solution.py:19
  19.5 0.6 gather_fusion.4
  20.1 1.3 copy.28
  21.4 3.0 %collective-permute-start.3 = (bf16[8,128,512]{1,2,0:T(8,128)(2,1)}, bf16[8,128,512]{1,2,0:T(8,128)(2,1)}, u32[]{:S(2)}, u32[]{:S(2)}) collective-permute-start(bf16[8,128,512]{1,2,0:T(8,128)(2,1)} %copy.28), channel_id=1, source_target_pairs={{0,16},{16,0},{2,18},{18,2},{4,20},{20,4},{6,22},{22,6},{8,24},{24... | collective-permute-start | bytes 3145736 | tf_op jit(solution)/shard_map/ppermute | solution.py:19
  24.4 0.0 copy-done.3
  24.4 0.1 copy.19
  24.5 0.1 reshape.155
  24.6 13.7 %gather_fusion = bf16[256,128,512]{2,1,0:T(8,128)(2,1)} fusion(bf16[8,128,512]{2,1,0:T(8,128)(2,1)S(1)} %copy-done, s32[1024]{0:T(1024)S(1)} %pad_clamp_fusion.4), kind=kCustom, calls=%fused_computation | custom fusion | bytes 67109888 | tf_op jit(solution)/shard_map/gather | solution.py:31
  38.3 21.4 %convolution_bitcast_fusion = f32[64,128,512]{1,2,0:T(8,128)} fusion(bf16[64,4,128,512]{3,2,1,0:T(8,128)(2,1)} %bitcast.48, bf16[64,4,128,128]{3,2,1,0:T(8,128)(2,1)} %param.7), kind=kOutput, calls=%fused_computation.12 | convolution fusion | flops 4294967296 | bytes 58720256 | tf_op jit(solution)/shard_map/fkab,fkbn->fan/dot_general | solution.py:32
  59.7 0.0 copy-start.4
  59.7 0.0 copy-start.2
  59.7 17.5 %copy.22 = f32[64,128,512]{2,1,0:T(8,128)} copy(f32[64,128,512]{1,2,0:T(8,128)} %convolution_bitcast_fusion) | data formatting | bytes 33554432 | tf_op jit(solution)/shard_map/fkab,fkbn->fan/dot_general | solution.py:32
  77.2 0.0 copy-done.4
  77.2 0.1 copy.30
  77.3 0.1 mul.28
  77.4 0.0 copy-done.2
  77.4 0.1 compare_select_fusion.2
  77.5 0.0 collective-permute-done
  77.5 1.7 %bitcast_reduce_fusion.3 = f32[2,128,512]{1,2,0:T(8,128)S(1)} fusion(bf16[8,128,512]{1,2,0:T(8,128)(2,1)} %collective-permute-done, bf16[32,128,128]{2,1,0:T(8,128)(2,1)} %param.10), kind=kOutput, calls=%fused_computation.16 | convolution fusion | flops 134610944 | bytes 1835008 | tf_op jit(solution)/shard_map/sab,sbn->san/dot_general | solution.py:37
  79.2 0.2 copy.23
  79.4 0.0 collective-permute-done.1
  79.5 1.7 %bitcast_reduce_fusion.2 = f32[2,128,512]{1,2,0:T(8,128)S(1)} fusion(bf16[8,128,512]{1,2,0:T(8,128)(2,1)} %collective-permute-done.1, bf16[32,128,128]{2,1,0:T(8,128)(2,1)} %param.10), kind=kOutput, calls=%fused_computation.15 | convolution fusion | flops 134610944 | bytes 1835008 | tf_op jit(solution)/shard_map/sab,sbn->san/dot_general | solution.py:37
  81.2 0.2 copy.25
  81.4 0.0 collective-permute-done.2
  81.4 1.7 %bitcast_reduce_fusion.1 = f32[2,128,512]{1,2,0:T(8,128)S(1)} fusion(bf16[8,128,512]{1,2,0:T(8,128)(2,1)} %collective-permute-done.2, bf16[32,128,128]{2,1,0:T(8,128)(2,1)} %param.10), kind=kOutput, calls=%fused_computation.14 | convolution fusion | flops 134610944 | bytes 1835008 | tf_op jit(solution)/shard_map/sab,sbn->san/dot_general | solution.py:37
  83.1 0.2 copy.27
  83.3 0.0 collective-permute-done.3
  83.4 1.7 %bitcast_reduce_fusion = f32[2,128,512]{1,2,0:T(8,128)S(1)} fusion(bf16[8,128,512]{1,2,0:T(8,128)(2,1)} %collective-permute-done.3, bf16[32,128,128]{2,1,0:T(8,128)(2,1)} %param.10), kind=kOutput, calls=%fused_computation.13 | convolution fusion | flops 134610944 | bytes 1835008 | tf_op jit(solution)/shard_map/sab,sbn->san/dot_general | solution.py:37
  85.1 0.2 copy.29
  85.3 2.5 %scatter_fusion = f32[64,128,512]{2,1,0:T(8,128)} fusion(f32[64,128,512]{2,1,0:T(8,128)} %copy.22, s32[2]{0:T(128)S(1)} %get-tuple-element.15, f32[2,128,512]{2,1,0:T(8,128)S(1)} %copy.23), kind=kCustom, calls=%fused_computation.5 | custom fusion | flops 131072 | bytes 1572872 | tf_op jit(solution)/shard_map/scatter-add | solution.py:43
  87.8 2.5 %scatter_fusion.1 = f32[64,128,512]{2,1,0:T(8,128)} fusion(f32[64,128,512]{2,1,0:T(8,128)} %scatter_fusion, s32[2]{0:T(128)S(1)} %get-tuple-element.14, f32[2,128,512]{2,1,0:T(8,128)S(1)} %copy.25), kind=kCustom, calls=%fused_computation.6 | custom fusion | flops 131072 | bytes 1572872 | tf_op jit(solution)/shard_map/scatter-add | solution.py:43
  90.4 2.6 %scatter_fusion.2 = f32[64,128,512]{2,1,0:T(8,128)} fusion(f32[64,128,512]{2,1,0:T(8,128)} %scatter_fusion.1, s32[2]{0:T(128)S(1)} %get-tuple-element.16, f32[2,128,512]{2,1,0:T(8,128)S(1)} %copy.27), kind=kCustom, calls=%fused_computation.7 | custom fusion | flops 131072 | bytes 1572872 | tf_op jit(solution)/shard_map/scatter-add | solution.py:43
  92.9 2.6 %scatter_fusion.3 = f32[64,128,512]{2,1,0:T(8,128)} fusion(f32[64,128,512]{2,1,0:T(8,128)} %scatter_fusion.2, s32[2]{0:T(128)S(1)} %get-tuple-element.13, f32[2,128,512]{2,1,0:T(8,128)S(1)} %copy.29), kind=kCustom, calls=%fused_computation.8 | custom fusion | flops 131072 | bytes 1572872 | tf_op jit(solution)/shard_map/scatter-add | solution.py:43
  95.5 0.0 copy-start.1
  95.5 10.0 %multiply_reduce_fusion = (f32[64,128]{1,0:T(8,128)}, f32[64,128]{1,0:T(8,128)}) fusion(f32[64,128,512]{2,1,0:T(8,128)} %scatter_fusion.3, f32[64,512]{1,0:T(8,128)S(1)} %bitcast.49), kind=kLoop, calls=%fused_computation.10 | loop fusion | flops 16760832 | bytes 16973824 | tf_op jit(solution)/shard_map/reduce_sum | solution.py:48
  105.5 0.0 all-reduce.3.cloned.1.call-update
  105.5 28.3 %all-reduce.3.cloned.1.call-done = (f32[64,128]{1,0:T(8,128)}, f32[64,128]{1,0:T(8,128)}) async-done(((f32[64,128]{1,0:T(8,128)}, f32[64,128]{1,0:T(8,128)}), (f32[64,128]{1,0:T(8,128)}, f32[64,128]{1,0:T(8,128)})) %all-reduce.3.cloned.1.call-update) | async-done | bytes 65552 | tf_op jit(solution)/shard_map/psum | solution.py:51
  133.8 0.8 add_divide_fusion
  134.6 9.5 %multiply_convert_fusion = bf16[64,128,512]{2,1,0:T(8,128)(2,1)} fusion(f32[64,128,512]{2,1,0:T(8,128)} %scatter_fusion.3, f32[64,128]{1,0:T(8,128)S(1)} %add_divide_fusion, f32[64,512]{1,0:T(8,128)S(1)} %bitcast.50), kind=kLoop, calls=%fused_computation.9 | loop fusion | flops 12582912 | bytes 25329664 | tf_op jit(solution)/shard_map/convert_element_type | solution.py:56
  144.1 0.0 copy-done.1
  (6 shorter events, 0.0 us)
Async XLA Ops:
  6.5 1.3 copy-start
  6.5 17.9 %copy-start.3 = (s32[64,4]{0,1:T(4,128)S(1)}, s32[64,4]{0,1:T(4,128)}, u32[]{:S(2)}) copy-start(s32[64,4]{0,1:T(4,128)} %param.8) | copy-start | bytes 3076
  6.5 127.3 %all-reduce.3.cloned.1.call-start = ((), (), s32[]{:S(2)}) async-start(), calls=%async_computation | async-start | bytes 131072 | tf_op jit(solution)/shard_map/psum | solution.py:51
  9.1 68.4 %collective-permute-start = (bf16[8,128,512]{1,2,0:T(8,128)(2,1)S(1)}, bf16[8,128,512]{1,2,0:T(8,128)(2,1)}, u32[]{:S(2)}, u32[]{:S(2)}) collective-permute-start(bf16[8,128,512]{1,2,0:T(8,128)(2,1)S(1)} %copy.21), channel_id=1, source_target_pairs={{0,2},{2,0},{4,6},{6,4},{8,10},{10,8},{12,14},{14,12},{16,18},{18,... | collective-permute-start | bytes 3145736 | tf_op jit(solution)/shard_map/ppermute | solution.py:19
  13.3 66.2 %collective-permute-start.1 = (bf16[8,128,512]{1,2,0:T(8,128)(2,1)}, bf16[8,128,512]{1,2,0:T(8,128)(2,1)}, u32[]{:S(2)}, u32[]{:S(2)}) collective-permute-start(bf16[8,128,512]{1,2,0:T(8,128)(2,1)} %copy.24), channel_id=1, source_target_pairs={{0,4},{4,0},{2,6},{6,2},{8,12},{12,8},{10,14},{14,10},{16,20},{20,... | collective-permute-start | bytes 3145736 | tf_op jit(solution)/shard_map/ppermute | solution.py:19
  17.8 63.6 %collective-permute-start.2 = (bf16[8,128,512]{1,2,0:T(8,128)(2,1)}, bf16[8,128,512]{1,2,0:T(8,128)(2,1)}, u32[]{:S(2)}, u32[]{:S(2)}) collective-permute-start(bf16[8,128,512]{1,2,0:T(8,128)(2,1)} %copy.26), channel_id=1, source_target_pairs={{0,8},{8,0},{2,10},{10,2},{4,12},{12,4},{6,14},{14,6},{16,24},{24,... | collective-permute-start | bytes 3145736 | tf_op jit(solution)/shard_map/ppermute | solution.py:19
  21.4 62.0 %collective-permute-start.3 = (bf16[8,128,512]{1,2,0:T(8,128)(2,1)}, bf16[8,128,512]{1,2,0:T(8,128)(2,1)}, u32[]{:S(2)}, u32[]{:S(2)}) collective-permute-start(bf16[8,128,512]{1,2,0:T(8,128)(2,1)} %copy.28), channel_id=1, source_target_pairs={{0,16},{16,0},{2,18},{18,2},{4,20},{20,4},{6,22},{22,6},{8,24},{24... | collective-permute-start | bytes 3145736 | tf_op jit(solution)/shard_map/ppermute | solution.py:19
  59.7 17.5 %copy-start.4 = (s32[64,4]{0,1:T(4,128)S(1)}, s32[64,4]{0,1:T(4,128)}, u32[]{:S(2)}) copy-start(s32[64,4]{0,1:T(4,128)} %param.13) | copy-start | bytes 3076
  59.7 17.7 %copy-start.2 = (s32[8]{0:T(128)S(1)}, s32[8]{0:T(128)}, u32[]{:S(2)}) copy-start(s32[8]{0:T(128)} %param.12) | copy-start | bytes 100
  95.5 48.6 %copy-start.1 = (bf16[8,128,512]{2,1,0:T(8,128)(2,1)S(1)}, bf16[8,128,512]{2,1,0:T(8,128)(2,1)}, u32[]{:S(2)}) copy-start(bf16[8,128,512]{2,1,0:T(8,128)(2,1)} %param.9) | copy-start | bytes 3145732
Sparse Core Ops, SparseCore 0:
  105.6 28.1 all-reduce.2
where the time goes:
time: 151 us
  local copies, waits for them, and re-layouts  39.9 us (26%)
  other arithmetic  31.4 us (21%)
  waiting for transfers between devices  28.4 us (19%)
  matrix products  28.3 us (19%)
  between operations  13.6 us (9%)
  starting transfers between devices  9.46 us (6%)
    psum x1, waiting for transfers between devices, on_device(): full, kept = lax.psum((full_part, kept_part), 'col')  28.3 us
    dot_general x1, matrix products, on_device(): jnp.einsum('fkab,fkbn->fan', first_interp, gathered, preferred_element_ty...  21.4 us
    dot_general x1, local copies, waits for them, and re-layouts, on_device(): jnp.einsum('fkab,fkbn->fan', first_interp, gathered, preferred_element_ty...  17.5 us
    gather x1, local copies, waits for them, and re-layouts, on_device(): gathered = second_interp[first_ids]  13.7 us
    scatter-add x4, other arithmetic, on_device(): raw = raw.at[target_table[bit_level]].add(grouped_all[bit_level])  10.2 us
    reduce_sum x1, other arithmetic, on_device(): jnp.sum(magnitude.reshape(fine_count, block_size, column_blocks, block_si...  9.96 us
    convert_element_type x1, other arithmetic, on_device(): return (kept_raw * scale[:, :, None]).astype(jnp.bfloat16)  9.49 us
    ppermute x4, starting transfers between devices, partner(): return lax.ppermute(block, axis, route)  9.46 us
  transfers between devices with their start and end apart: 5, of which 1 were waited for; matrix products, arithmetic and copies ran while one was open for 43% of the time, Pallas kernels for 0%

commit v1 on v0

v1 whole, which is shorter than its diff:
```python
import functools

import jax
import jax.numpy as jnp
from jax import lax
from jax.experimental import pallas as pl
from jax.experimental.pallas import tpu as pltpu
from jax.sharding import PartitionSpec as P

G = 4
LEVELS = 4
GROUPS = 2
CHUNK = 8
WAVES = ((3, 1), (0, 2))
epsilon = 1e-06
VMEM_SCOPED = 14 * 2**20
SMEM_SPEC = pl.BlockSpec(memory_space=pltpu.SMEM)
VMEM_SPEC = pl.BlockSpec(memory_space=pltpu.VMEM)
HBM_SPEC = pl.BlockSpec(memory_space=pltpu.HBM)
ANY_SPEC = pl.BlockSpec(memory_space=pl.ANY)


def lanes():
    return lax.broadcasted_iota(jnp.int32, (128, 128), 1)


def level_of(wave, core):
    first, second = WAVES[wave]
    return jnp.where(core == 0, first, second)


def row_sums(block, weights):
    full = kept = None
    for column in range(4):
        part = jnp.abs(block[:, column * 128 : (column + 1) * 128])
        weighted = part * weights[column]
        full = part if full is None else full + part
        kept = weighted if kept is None else kept + weighted
    return jnp.sum(full, axis=1, keepdims=True), jnp.sum(kept, axis=1, keepdims=True)


def weights_of(mask, block):
    return [mask[column, block].astype(jnp.float32) for column in range(4)]


def inner_block(ids, mask, block, first, second, raw, sums):
    left = jnp.concatenate([first[k] for k in range(4)], axis=1)
    right = jnp.concatenate([second[ids[k, block]] for k in range(4)], axis=0)
    product = jnp.dot(left, right, preferred_element_type=jnp.float32)
    raw[block] = product
    full, kept = row_sums(product, weights_of(mask, block))
    lane = lanes()
    sums[...] = jnp.where(lane == block, full, jnp.where(lane == block + 64, kept, sums[...]))


def pick_level(wave, by_level, out, sem):
    copy = pltpu.make_async_copy(by_level.at[level_of(wave, lax.axis_index("col"))], out, sem)
    copy.start()
    copy.wait()


def inner_head(
    count, tables_hbm, first_hbm, second_hbm, tables, raw, sums, rest, second, head, table_sem, first_sem, rest_sem, second_sem
):
    total = first_hbm.shape[0]
    ids, mask = tables[:2]
    table_copies = [
        pltpu.make_async_copy(source, target, table_sem.at[place])
        for place, (source, target) in enumerate(zip(tables_hbm, tables))
    ]
    for copy in table_copies:
        copy.start()

    def first_copy(chunk):
        span = pl.ds(chunk * CHUNK, CHUNK)
        return pltpu.make_async_copy(first_hbm.at[span], head.at[span], first_sem.at[chunk])

    rest_copy = pltpu.make_async_copy(first_hbm.at[pl.ds(count, total - count)], rest, rest_sem)
    second_copy = pltpu.make_async_copy(second_hbm, second, second_sem)
    second_copy.start()
    for chunk in range(count // CHUNK):
        first_copy(chunk).start()
    rest_copy.start()
    sums[...] = jnp.zeros_like(sums)
    for copy in table_copies:
        copy.wait()
    second_copy.wait()

    @pl.loop(0, count // CHUNK)
    def _(chunk):
        first_copy(chunk).wait()
        for j in range(CHUNK):
            block = chunk * CHUNK + j
            inner_block(ids, mask, block, head.at[block], second, raw, sums)

    rest_copy.wait()


def inner_rest(start, ids, mask, rest, second, raw_in, sums_in, after, raw, sums):
    del raw_in, after
    sums[...] = sums_in[...]

    @pl.loop(0, rest.shape[0] // CHUNK)
    def _(chunk):
        for j in range(CHUNK):
            place = chunk * CHUNK + j
            inner_block(ids, mask, start + place, rest.at[place], second, raw, sums)


def coupling_products(wave, send_rows, tiles, second, second_other, after, out_own, out_other):
    del after
    level = level_of(wave, lax.axis_index("col"))
    for group in range(GROUPS):
        left = jnp.concatenate([tiles[group * G + s] for s in range(G)], axis=1)
        for rows, out in ((second, out_own), (second_other, out_other)):
            right = jnp.concatenate([rows[send_rows[level, group * G + s]] for s in range(G)], axis=0)
            product = jnp.dot(left, right, preferred_element_type=jnp.float32)
            top = jnp.max(jnp.abs(product), axis=1, keepdims=True)
            power = jnp.floor(jnp.log(jnp.maximum(top, 2.0**-100)) * 1.4426950408889634) + 1.0
            scaled = jnp.round(product * jnp.exp2(15.0 - power))
            coded = jnp.clip(scaled, -32767.0, 32767.0).astype(jnp.int32).astype(jnp.int16)
            for column in range(4):
                out[pl.ds((group * 4 + column) * 128, 128), :] = coded[:, column * 128 : (column + 1) * 128]
            turned = jnp.broadcast_to(power, (128, 128)).T
            out[pl.ds(1024 + 16 * group, 16), :] = turned[:16].astype(jnp.int32).astype(jnp.int16)


def scale_all(mask, raw, sums, sums_other, out_hbm, done, out, sem):
    done[...] = jnp.zeros_like(done)
    both = sums[...] + sums_other[...]
    scale = both[:, :64] / (both[:, 64:] + epsilon)
    scale = jnp.concatenate([scale, scale], axis=1)

    def out_copy(chunk):
        span = pl.ds(chunk * CHUNK, CHUNK)
        return pltpu.make_async_copy(out.at[span], out_hbm.at[span], sem.at[chunk])

    chunks = raw.shape[0] // CHUNK

    @pl.loop(0, chunks)
    def _(chunk):
        for j in range(CHUNK):
            block = chunk * CHUNK + j
            factor = jnp.take_along_axis(scale, jnp.full((128, 128), block, jnp.int32), axis=1)
            weights = weights_of(mask, block)
            for column in range(4):
                span = slice(column * 128, (column + 1) * 128)
                out[block, :, span] = (raw[block, :, span] * (factor * weights[column])).astype(jnp.bfloat16)
        out_copy(chunk).start()

    for chunk in range(chunks):
        out_copy(chunk).wait()


def add_products(targets, mask, raw_in, same_a, cross_a, same_b, cross_b, after, raw, final, sums):
    del raw_in, after
    core = lax.axis_index("col")
    for place, source in enumerate((same_a, cross_a, same_b, cross_b)):
        level = level_of(place // 2, core if place % 2 == 0 else 1 - core)
        for group in range(GROUPS):
            block = targets[level * GROUPS + group]
            power = source[pl.ds(1024 + 16 * group, 16), :].astype(jnp.int32).astype(jnp.float32)
            step = jnp.exp2(jnp.concatenate([power] * 8, axis=0).T - 15.0)
            for column in range(4):
                span = slice(column * 128, (column + 1) * 128)
                coded = source[pl.ds((group * 4 + column) * 128, 128), :].astype(jnp.int32)
                raw[block, :, span] += coded.astype(jnp.float32) * step
    lane = lanes()
    found = jnp.zeros((128, 128), jnp.float32)
    for entry in range(LEVELS * GROUPS):
        block = targets[entry]
        weights = weights_of(mask, block)
        product = raw[block]
        full, kept = row_sums(product, weights)
        found = jnp.where(lane == entry, full, jnp.where(lane == entry + 64, kept, found))
        for column in range(4):
            span = slice(column * 128, (column + 1) * 128)
            final[entry, :, span] = product[:, span] * weights[column]
    sums[...] = found


def scale_final(targets, final, sums, sums_other, out_in, out_hbm, out, sem):
    del out_in
    both = sums[...] + sums_other[...]
    scale = both[:, :64] / (both[:, 64:] + epsilon)
    blocks = [targets[entry] for entry in range(LEVELS * GROUPS)]
    latest = []
    for entry, block in enumerate(blocks):
        again = jnp.bool_(False)
        for later in blocks[entry + 1 :]:
            again = again | (later == block)
        latest.append(jnp.logical_not(again))

    def out_copy(entry):
        return pltpu.make_async_copy(out.at[entry], out_hbm.at[blocks[entry]], sem.at[entry])

    for entry in range(LEVELS * GROUPS):
        factor = jnp.broadcast_to(scale[:, entry : entry + 1], (128, 128))
        for column in range(4):
            span = slice(column * 128, (column + 1) * 128)
            out[entry, :, span] = (final[entry, :, span] * factor).astype(jnp.bfloat16)
        pl.when(latest[entry])(lambda entry=entry: out_copy(entry).start())
    for entry in range(LEVELS * GROUPS):
        pl.when(latest[entry])(lambda entry=entry: out_copy(entry).wait())


def call(kernel, name, outs, in_specs, out_specs, scratch=(), aliases=None):
    return pl.pallas_call(
        kernel,
        out_shape=outs,
        in_specs=in_specs,
        out_specs=out_specs,
        scratch_shapes=list(scratch),
        input_output_aliases=aliases or {},
        compiler_params=pltpu.CompilerParams(vmem_limit_bytes=VMEM_SCOPED),
        cost_estimate=pl.CostEstimate(flops=1, bytes_accessed=1, transcendentals=0),
        name=name,
    )


def route(count, wave, swap):
    pairs = []
    for domain in range(count):
        for core in range(2):
            other = domain ^ (1 << WAVES[wave][core])
            pairs.append((domain * 2 + core, other * 2 + (core ^ swap)))
    return pairs


def in_hbm(array):
    return pltpu.with_memory_space_constraint(array, pltpu.HBM)


def swap_cores(block):
    return lax.ppermute(block, "col", [(0, 1), (1, 0)])


def on_device(first_interp, first_ids, second_interp, coupling, send_rows, targets, keep_mask):
    fine = first_interp.shape[0]
    head = 24
    core = lax.axis_index("col")
    count = lax.axis_size("dom")
    by_level = in_hbm(coupling.reshape(LEVELS, 8, 128, 128))
    tiles = []
    for wave in range(2):
        own = call(
            functools.partial(pick_level, wave),
            "pick_level",
            pltpu.VMEM((8, 128, 128), jnp.bfloat16),
            [HBM_SPEC],
            VMEM_SPEC,
            [pltpu.SemaphoreType.DMA],
        )(by_level)
        tiles.append(lax.ppermute(own, ("dom", "col"), route(count, wave, 0)))
    second_other = swap_cores(second_interp)

    tables = [in_hbm(x) for x in (first_ids.T, keep_mask.T, send_rows, targets)]
    raw_shape = pltpu.VMEM((fine, 128, 512), jnp.float32)
    sums_shape = pltpu.VMEM((128, 128), jnp.float32)
    tables, raw, sums, rest, second = call(
        functools.partial(inner_head, head),
        "inner_head",
        (
            [pltpu.SMEM(x.shape, x.dtype) for x in tables],
            raw_shape,
            sums_shape,
            pltpu.VMEM((fine - head, 4, 128, 128), jnp.bfloat16),
            pltpu.VMEM((8, 128, 512), jnp.bfloat16),
        ),
        [[HBM_SPEC] * 4, HBM_SPEC, HBM_SPEC],
        ([SMEM_SPEC] * 4,) + (VMEM_SPEC,) * 4,
        [
            pltpu.VMEM((head, 4, 128, 128), jnp.bfloat16),
            pltpu.SemaphoreType.DMA((4,)),
            pltpu.SemaphoreType.DMA((head // CHUNK,)),
            pltpu.SemaphoreType.DMA,
            pltpu.SemaphoreType.DMA,
        ],
    )(tables, in_hbm(first_interp), in_hbm(second_interp))
    ids, mask, send_rows, targets = tables

    def products(wave, after):
        return call(
            functools.partial(coupling_products, wave),
            "coupling_products",
            (pltpu.VMEM((1056, 128), jnp.int16),) * 2,
            [SMEM_SPEC, VMEM_SPEC, VMEM_SPEC, VMEM_SPEC, ANY_SPEC],
            (VMEM_SPEC,) * 2,
        )(send_rows, tiles[wave], second, second_other, after)

    def deliver(wave, own, other):
        return (
            lax.ppermute(own, ("dom", "col"), route(count, wave, 0)),
            lax.ppermute(other, ("dom", "col"), route(count, wave, 1)),
        )

    own_a, other_a = products(0, sums)
    same_a, cross_a = deliver(0, own_a, other_a)
    own_b, other_b = products(1, own_a)
    same_b, cross_b = deliver(1, own_b, other_b)

    raw, sums = call(
        functools.partial(inner_rest, head),
        "inner_rest",
        (raw_shape, sums_shape),
        [SMEM_SPEC, SMEM_SPEC, VMEM_SPEC, VMEM_SPEC, VMEM_SPEC, VMEM_SPEC, ANY_SPEC],
        (VMEM_SPEC,) * 2,
        aliases={4: 0, 5: 1},
    )(ids, mask, rest, second, raw, sums, own_b)

    out, done = call(
        scale_all,
        "scale_all",
        (jax.ShapeDtypeStruct((fine, 128, 512), jnp.bfloat16), pltpu.VMEM((8, 128), jnp.float32)),
        [SMEM_SPEC, VMEM_SPEC, VMEM_SPEC, VMEM_SPEC],
        (HBM_SPEC, VMEM_SPEC),
        [pltpu.VMEM((fine, 128, 512), jnp.bfloat16), pltpu.SemaphoreType.DMA((fine // CHUNK,))],
    )(mask, raw, sums, swap_cores(sums))

    _, final, sums = call(
        add_products,
        "add_products",
        (raw_shape, pltpu.VMEM((8, 128, 512), jnp.float32), sums_shape),
        [SMEM_SPEC, SMEM_SPEC] + [VMEM_SPEC] * 6,
        (VMEM_SPEC,) * 3,
        aliases={2: 0},
    )(targets, mask, raw, same_a, cross_a, same_b, cross_b, done)
    return call(
        scale_final,
        "scale_final",
        jax.ShapeDtypeStruct((fine, 128, 512), jnp.bfloat16),
        [SMEM_SPEC, VMEM_SPEC, VMEM_SPEC, VMEM_SPEC, HBM_SPEC],
        HBM_SPEC,
        [pltpu.VMEM((8, 128, 512), jnp.bfloat16), pltpu.SemaphoreType.DMA((8,))],
        aliases={4: 0},
    )(targets, final, sums, swap_cores(sums), out)


def solution(mesh):
    return jax.shard_map(
        on_device,
        mesh=mesh,
        in_specs=(
            P("dom", None, None, None),
            P("dom", None),
            P("dom", None, "col"),
            P("dom", None, None),
            P("dom", None),
            P("dom"),
            P("dom", "col"),
        ),
        out_specs=P("dom", None, "col"),
        check_vma=False,
    )
```

time: 151 us -> 36.5 us (0.24)
  local copies, waits for them, and re-layouts: 39.9 us -> 0 us
  other arithmetic: 31.4 us -> 0 us
  matrix products: 28.3 us -> 0 us
  waiting for transfers between devices: 28.4 us -> 3.82 us
  Pallas kernels: 0 us -> 17.6 us
  between operations: 13.6 us -> 0.1 us
  starting transfers between devices: 9.46 us -> 14.9 us
    psum x1 -> x0, waiting for transfers between devices: 28.3 us -> none  [on_device(): full, kept = lax.psum((full_part, kept_part), 'col')]
    dot_general x5 -> x0, matrix products: 28.3 us -> none  [the longest x1 21.4 us: on_device(): jnp.einsum('fkab,fkbn->fan', first_interp, gathered, preferred_element_ty...]
    gather x9 -> x0, local copies, waits for them, and re-layouts: 20.7 us -> none  [the longest x1 13.7 us: on_device(): gathered = second_interp[first_ids]]
    pallas_call x0 -> x9, Pallas kernels: none -> 17.6 us  [the longest x1 4.39 us: on_device(): call(functools.partial(inner_head, head), 'inner_head', ([pltpu.SMEM(x.sh...]
    dot_general x1 -> x0, local copies, waits for them, and re-layouts: 17.5 us -> none  [on_device(): jnp.einsum('fkab,fkbn->fan', first_interp, gathered, preferred_element_ty...]
    scatter-add x4 -> x0, other arithmetic: 10.2 us -> none  [on_device(): raw = raw.at[target_table[bit_level]].add(grouped_all[bit_level])]
    reduce_sum x1 -> x0, other arithmetic: 9.96 us -> none  [on_device(): jnp.sum(magnitude.reshape(fine_count, block_size, column_blocks, block_si...]
    convert_element_type x2 -> x0, other arithmetic: 9.49 us -> none  [the longest x1 9.49 us: on_device(): return (kept_raw * scale[:, :, None]).astype(jnp.bfloat16)]
  transfers between devices with their start and end apart: 5 -> 9, of which waited for: 1 -> 4; matrix products, arithmetic and copies ran while one was open for 43% -> 0% of each run, Pallas kernels for 0% -> 41%
where the time goes in v1:
time: 36.5 us; the launch traced here: 36.4 us
  Pallas kernels  17.6 us (48%)
  starting transfers between devices  14.9 us (41%)
  waiting for transfers between devices  3.82 us (10%)
    ppermute x3, starting transfers between devices, swap_cores(): return lax.ppermute(block, 'col', [(0, 1), (1, 0)])  6.9 us
    pallas_call x1, Pallas kernels, on_device(): call(functools.partial(inner_head, head), 'inner_head', ([pltpu.SMEM(x.sh...  4.39 us
    pallas_call x1, Pallas kernels, on_device(): call(functools.partial(inner_rest, head), 'inner_rest', (raw_shape, sums_...  4.08 us
    pallas_call x1, Pallas kernels, on_device(): call(scale_all, 'scale_all', (jax.ShapeDtypeStruct((fine, 128, 512), jnp....  3.83 us
    ppermute x2, starting transfers between devices, deliver(): lax.ppermute(own, ('dom', 'col'), route(count, wave, 0))  3.23 us
    ppermute x2, starting transfers between devices, on_device(): tiles.append(lax.ppermute(own, ('dom', 'col'), route(count, wave, 0)))  2.99 us
    ppermute x3, waiting for transfers between devices, swap_cores(): return lax.ppermute(block, 'col', [(0, 1), (1, 0)])  2.15 us
    pallas_call x2, Pallas kernels, on_device(): call(functools.partial(pick_level, wave), 'pick_level', pltpu.VMEM((8, 12...  1.91 us
  transfers between devices with their start and end apart: 9, of which 4 were waited for; matrix products, arithmetic and copies ran while one was open for 0% of the time, Pallas kernels for 41%

profile of v1, /device:TPU:1, one launch (start us, length us, event | category | flops | bytes accessed | tf_op | source)
XLA Modules:
  0.0 36.4 jit_solution(8479437746768952557)
XLA Ops:
  0.0 3.2 %collective-permute-start.1 = (bf16[8,128,512]{2,1,0:T(8,128)(2,1)}, bf16[8,128,512]{2,1,0:T(8,128)(2,1)S(1)}, u32[]{:S(2)}, u32[]{:S(2)}) collective-permute-start(bf16[8,128,512]{2,1,0:T(8,128)(2,1)} %second_hbm.1), channel_id=1, source_target_pairs={{0,1},{1,0},{2,3},{3,2},{4,5},{5,4},{6,7},{7,6},{8,9},{9,8},{10,11... | collective-permute-start | bytes 3145736 | tf_op jit(solution)/shard_map/ppermute | solution.py:235
  3.2 1.0 %pick_level.3 = bf16[8,128,128]{2,1,0:T(8,128)(2,1)S(1)} custom-call(bf16[4,8,128,128]{3,2,1,0:T(8,128)(2,1)} %bitcast.3), custom_call_target="tpu_custom_call" | custom-call | flops 1 | bytes 1 | tf_op jit(solution)/shard_map/pick_level/pallas_call | solution.py:246
  4.2 1.3 %collective-permute-start.2 = (bf16[8,128,128]{2,1,0:T(8,128)(2,1)S(1)}, bf16[8,128,128]{2,1,0:T(8,128)(2,1)S(1)}, u32[]{:S(2)}, u32[]{:S(2)}) collective-permute-start(bf16[8,128,128]{2,1,0:T(8,128)(2,1)S(1)} %pick_level.3), channel_id=1, source_target_pairs={{0,16},{1,5},{2,18},{3,7},{4,20},{5,1},{6,22},{7,3},{8,24},{9,13},... | collective-permute-start | bytes 786440 | tf_op jit(solution)/shard_map/ppermute | solution.py:254
  5.5 1.0 %pick_level.2 = bf16[8,128,128]{2,1,0:T(8,128)(2,1)S(1)} custom-call(bf16[4,8,128,128]{3,2,1,0:T(8,128)(2,1)} %bitcast.4), custom_call_target="tpu_custom_call" | custom-call | flops 1 | bytes 1 | tf_op jit(solution)/shard_map/pick_level/pallas_call | solution.py:246
  6.4 1.7 %collective-permute-start = (bf16[8,128,128]{2,1,0:T(8,128)(2,1)S(1)}, bf16[8,128,128]{2,1,0:T(8,128)(2,1)S(1)}, u32[]{:S(2)}, u32[]{:S(2)}) collective-permute-start(bf16[8,128,128]{2,1,0:T(8,128)(2,1)S(1)} %pick_level.2), channel_id=1, source_target_pairs={{0,2},{1,9},{2,0},{3,11},{4,6},{5,13},{6,4},{7,15},{8,10},{9,1},{1... | collective-permute-start | bytes 786440 | tf_op jit(solution)/shard_map/ppermute | solution.py:254
  8.2 4.4 %inner_head.1 = (s32[4,64]{1,0:T(4,128)S(4)}, s32[4,64]{1,0:T(4,128)S(4)}, s32[4,8]{1,0:T(4,128)S(4)}, s32[8]{0:T(128)S(4)}, f32[64,128,512]{2,1,0:T(8,128)S(1)}...) custom-call(s32[4,64]{1,0:T(4,128)} %bitcast.5, ...), custom_call_target="tpu_custom_call" | custom-call | flops 1 | bytes 1 | tf_op jit(solution)/shard_map/inner_head/pallas_call | solution.py:260
  12.6 0.0 collective-permute-done.2.tiles
  12.6 0.0 collective-permute-done.1.second_other
  12.6 0.6 %coupling_products.2 = (s16[1056,128]{1,0:T(8,128)(2,1)S(1)}, s16[1056,128]{1,0:T(8,128)(2,1)S(1)}) custom-call(s32[4,8]{1,0:T(4,128)S(4)} %get-tuple-element.30.send_rows, bf16[8,128,128]{2,1,0:T(8,128)(2,1)S(1)} %collective-permute-done.2.tiles, bf16[8,128,512]{2,1,0:T(8,128)(2,1)S(1)} %get-tuple-element.27.second, ...), custom_call_target="tpu_custom_call" | custom-call | flops 1 | bytes 1 | tf_op jit(solution)/shard_map/coupling_products/pallas_call | solution.py:283
  13.2 1.4 %collective-permute-done.tiles = bf16[8,128,128]{2,1,0:T(8,128)(2,1)S(1)} collective-permute-done((bf16[8,128,128]{2,1,0:T(8,128)(2,1)S(1)}, bf16[8,128,128]{2,1,0:T(8,128)(2,1)S(1)}, u32[]{:S(2)}, u32[]{:S(2)}) %collective-permute-start) | collective-permute-done | bytes 262176 | tf_op jit(solution)/shard_map/ppermute | solution.py:254
  14.6 0.6 %coupling_products.3 = (s16[1056,128]{1,0:T(8,128)(2,1)S(1)}, s16[1056,128]{1,0:T(8,128)(2,1)S(1)}) custom-call(s32[4,8]{1,0:T(4,128)S(4)} %get-tuple-element.30.send_rows, bf16[8,128,128]{2,1,0:T(8,128)(2,1)S(1)} %collective-permute-done.tiles, bf16[8,128,512]{2,1,0:T(8,128)(2,1)S(1)} %get-tuple-element.27.second, ...), custom_call_target="tpu_custom_call" | custom-call | flops 1 | bytes 1 | tf_op jit(solution)/shard_map/coupling_products/pallas_call | solution.py:283
  15.2 0.5 %collective-permute-start.6 = (s16[1056,128]{1,0:T(8,128)(2,1)S(1)}, s16[1056,128]{1,0:T(8,128)(2,1)S(1)}, u32[]{:S(2)}, u32[]{:S(2)}) collective-permute-start(s16[1056,128]{1,0:T(8,128)(2,1)S(1)} %get-tuple-element.35), channel_id=1, source_target_pairs={{0,3},{1,8},{2,1},{3,10},{4,7},{5,12},{6,5},{7,14},{8,11},{9,0},{1... | collective-permute-start | bytes 811016 | tf_op jit(solution)/shard_map/ppermute | solution.py:294
  15.7 1.4 %collective-permute-start.5 = (s16[1056,128]{1,0:T(8,128)(2,1)S(1)}, s16[1056,128]{1,0:T(8,128)(2,1)S(1)}, u32[]{:S(2)}, u32[]{:S(2)}) collective-permute-start(s16[1056,128]{1,0:T(8,128)(2,1)S(1)} %get-tuple-element.32.after), channel_id=1, source_target_pairs={{0,2},{1,9},{2,0},{3,11},{4,6},{5,13},{6,4},{7,15},{8,10},{9,1},{1... | collective-permute-start | bytes 811016 | tf_op jit(solution)/shard_map/ppermute | solution.py:293
  17.1 1.4 %collective-permute-start.4 = (s16[1056,128]{1,0:T(8,128)(2,1)S(1)}, s16[1056,128]{1,0:T(8,128)(2,1)S(1)}, u32[]{:S(2)}, u32[]{:S(2)}) collective-permute-start(s16[1056,128]{1,0:T(8,128)(2,1)S(1)} %get-tuple-element.34), channel_id=1, source_target_pairs={{0,17},{1,4},{2,19},{3,6},{4,21},{5,0},{6,23},{7,2},{8,25},{9,12},... | collective-permute-start | bytes 811016 | tf_op jit(solution)/shard_map/ppermute | solution.py:294
  18.5 1.8 %collective-permute-start.3 = (s16[1056,128]{1,0:T(8,128)(2,1)S(1)}, s16[1056,128]{1,0:T(8,128)(2,1)S(1)}, u32[]{:S(2)}, u32[]{:S(2)}) collective-permute-start(s16[1056,128]{1,0:T(8,128)(2,1)S(1)} %get-tuple-element.31.after), channel_id=1, source_target_pairs={{0,16},{1,5},{2,18},{3,7},{4,20},{5,1},{6,22},{7,3},{8,24},{9,13},... | collective-permute-start | bytes 811016 | tf_op jit(solution)/shard_map/ppermute | solution.py:293
  20.3 4.1 %inner_rest.1 = (f32[64,128,512]{2,1,0:T(8,128)S(1)}, f32[128,128]{1,0:T(8,128)S(1)}) custom-call(s32[4,64]{1,0:T(4,128)S(4)} %get-tuple-element.25.ids, s32[4,64]{1,0:T(4,128)S(4)} %get-tuple-element.24.mask, bf16[40,4,128,128]{3,2,1,0:T(8,128)(2,1)S(1)} %get-tuple-element.26.rest, ...), custom_call_target="tpu_custom_call", output_to_operand_aliasing={{0}: (4, {}), {1}: (5, {})} | custom-call | flops 1 | bytes 1 | tf_op jit(solution)/shard_map/inner_rest/pallas_call | solution.py:302
  24.4 0.1 collective-permute-start.7
  24.5 1.2 %collective-permute-done.7.sums_other = f32[128,128]{1,0:T(8,128)S(1)} collective-permute-done((f32[128,128]{1,0:T(8,128)S(1)}, f32[128,128]{1,0:T(8,128)S(1)}, u32[]{:S(2)}, u32[]{:S(2)}) %collective-permute-start.7) | collective-permute-done | bytes 65568 | tf_op jit(solution)/shard_map/ppermute | solution.py:235
  25.7 3.8 %scale_all.1 = (bf16[64,128,512]{2,1,0:T(8,128)(2,1)}, f32[8,128]{1,0:T(8,128)S(1)}) custom-call(s32[4,64]{1,0:T(4,128)S(4)} %get-tuple-element.24.mask, f32[64,128,512]{2,1,0:T(8,128)S(1)} %get-tuple-element.33.raw.raw_in, f32[128,128]{1,0:T(8,128)S(1)} %get-tuple-element.36.sums, f32[128,128]{1,0:T(8,128)S(1)} %collective-permute-done.7.sums_other), custom_call_target="tpu_custom_call" | custom-call | flops 1 | bytes 1 | tf_op jit(solution)/shard_map/scale_all/pallas_call | solution.py:311
  29.6 0.0 collective-permute-done.6.cross_b
  29.6 0.0 collective-permute-done.5.same_b
  29.6 0.0 collective-permute-done.4.cross_a
  29.6 0.2 collective-permute-done.3.same_a
  29.8 0.9 %add_products.1 = (f32[64,128,512]{2,1,0:T(8,128)S(1)}, f32[8,128,512]{2,1,0:T(8,128)S(1)}, f32[128,128]{1,0:T(8,128)S(1)}) custom-call(s32[8]{0:T(128)S(4)} %get-tuple-element.23.targets, s32[4,64]{1,0:T(4,128)S(4)} %get-tuple-element.24.mask, f32[64,128,512]{2,1,0:T(8,128)S(1)} %get-tuple-element.33.raw.raw_in, ...), custom_call_target="tpu_custom_call", output_to_operand_aliasing={{0}: (2, {})} | custom-call | flops 1 | bytes 1 | tf_op jit(solution)/shard_map/add_products/pallas_call | solution.py:320
  30.8 3.6 %collective-permute-start.8 = (f32[128,128]{1,0:T(8,128)S(1)}, f32[128,128]{1,0:T(8,128)S(1)}, u32[]{:S(2)}, u32[]{:S(2)}) collective-permute-start(f32[128,128]{1,0:T(8,128)S(1)} %get-tuple-element.39.sums), channel_id=1, source_target_pairs={{0,1},{1,0},{2,3},{3,2},{4,5},{5,4},{6,7},{7,6},{8,9},{9,8},{10,11... | collective-permute-start | bytes 196616 | tf_op jit(solution)/shard_map/ppermute | solution.py:235
  34.3 0.9 %collective-permute-done.8.sums_other = f32[128,128]{1,0:T(8,128)S(1)} collective-permute-done((f32[128,128]{1,0:T(8,128)S(1)}, f32[128,128]{1,0:T(8,128)S(1)}, u32[]{:S(2)}, u32[]{:S(2)}) %collective-permute-start.8) | collective-permute-done | bytes 65568 | tf_op jit(solution)/shard_map/ppermute | solution.py:235
  35.2 1.2 %scale_final.1 = bf16[64,128,512]{2,1,0:T(8,128)(2,1)} custom-call(s32[8]{0:T(128)S(4)} %get-tuple-element.23.targets, f32[8,128,512]{2,1,0:T(8,128)S(1)} %get-tuple-element.38.final, f32[128,128]{1,0:T(8,128)S(1)} %get-tuple-element.39.sums, f32[128,128]{1,0:T(8,128)S(1)} %collective-permute-done.8.sums_other, ...), custom_call_target="tpu_custom_call", output_to_operand_aliasing={{}: (4, {})} | custom-call | flops 1 | bytes 1 | tf_op jit(solution)/shard_map/scale_final/pallas_call | solution.py:328
Async XLA Ops:
  0.0 12.6 %collective-permute-start.1 = (bf16[8,128,512]{2,1,0:T(8,128)(2,1)}, bf16[8,128,512]{2,1,0:T(8,128)(2,1)S(1)}, u32[]{:S(2)}, u32[]{:S(2)}) collective-permute-start(bf16[8,128,512]{2,1,0:T(8,128)(2,1)} %second_hbm.1), channel_id=1, source_target_pairs={{0,1},{1,0},{2,3},{3,2},{4,5},{5,4},{6,7},{7,6},{8,9},{9,8},{10,11... | collective-permute-start | bytes 3145736 | tf_op jit(solution)/shard_map/ppermute | solution.py:235
  4.2 8.4 %collective-permute-start.2 = (bf16[8,128,128]{2,1,0:T(8,128)(2,1)S(1)}, bf16[8,128,128]{2,1,0:T(8,128)(2,1)S(1)}, u32[]{:S(2)}, u32[]{:S(2)}) collective-permute-start(bf16[8,128,128]{2,1,0:T(8,128)(2,1)S(1)} %pick_level.3), channel_id=1, source_target_pairs={{0,16},{1,5},{2,18},{3,7},{4,20},{5,1},{6,22},{7,3},{8,24},{9,13},... | collective-permute-start | bytes 786440 | tf_op jit(solution)/shard_map/ppermute | solution.py:254
  6.4 8.2 %collective-permute-start = (bf16[8,128,128]{2,1,0:T(8,128)(2,1)S(1)}, bf16[8,128,128]{2,1,0:T(8,128)(2,1)S(1)}, u32[]{:S(2)}, u32[]{:S(2)}) collective-permute-start(bf16[8,128,128]{2,1,0:T(8,128)(2,1)S(1)} %pick_level.2), channel_id=1, source_target_pairs={{0,2},{1,9},{2,0},{3,11},{4,6},{5,13},{6,4},{7,15},{8,10},{9,1},{1... | collective-permute-start | bytes 786440 | tf_op jit(solution)/shard_map/ppermute | solution.py:254
  15.2 14.3 %collective-permute-start.6 = (s16[1056,128]{1,0:T(8,128)(2,1)S(1)}, s16[1056,128]{1,0:T(8,128)(2,1)S(1)}, u32[]{:S(2)}, u32[]{:S(2)}) collective-permute-start(s16[1056,128]{1,0:T(8,128)(2,1)S(1)} %get-tuple-element.35), channel_id=1, source_target_pairs={{0,3},{1,8},{2,1},{3,10},{4,7},{5,12},{6,5},{7,14},{8,11},{9,0},{1... | collective-permute-start | bytes 811016 | tf_op jit(solution)/shard_map/ppermute | solution.py:294
  15.7 13.9 %collective-permute-start.5 = (s16[1056,128]{1,0:T(8,128)(2,1)S(1)}, s16[1056,128]{1,0:T(8,128)(2,1)S(1)}, u32[]{:S(2)}, u32[]{:S(2)}) collective-permute-start(s16[1056,128]{1,0:T(8,128)(2,1)S(1)} %get-tuple-element.32.after), channel_id=1, source_target_pairs={{0,2},{1,9},{2,0},{3,11},{4,6},{5,13},{6,4},{7,15},{8,10},{9,1},{1... | collective-permute-start | bytes 811016 | tf_op jit(solution)/shard_map/ppermute | solution.py:293
  17.1 12.5 %collective-permute-start.4 = (s16[1056,128]{1,0:T(8,128)(2,1)S(1)}, s16[1056,128]{1,0:T(8,128)(2,1)S(1)}, u32[]{:S(2)}, u32[]{:S(2)}) collective-permute-start(s16[1056,128]{1,0:T(8,128)(2,1)S(1)} %get-tuple-element.34), channel_id=1, source_target_pairs={{0,17},{1,4},{2,19},{3,6},{4,21},{5,0},{6,23},{7,2},{8,25},{9,12},... | collective-permute-start | bytes 811016 | tf_op jit(solution)/shard_map/ppermute | solution.py:294
  18.5 11.4 %collective-permute-start.3 = (s16[1056,128]{1,0:T(8,128)(2,1)S(1)}, s16[1056,128]{1,0:T(8,128)(2,1)S(1)}, u32[]{:S(2)}, u32[]{:S(2)}) collective-permute-start(s16[1056,128]{1,0:T(8,128)(2,1)S(1)} %get-tuple-element.31.after), channel_id=1, source_target_pairs={{0,16},{1,5},{2,18},{3,7},{4,20},{5,1},{6,22},{7,3},{8,24},{9,13},... | collective-permute-start | bytes 811016 | tf_op jit(solution)/shard_map/ppermute | solution.py:293
  24.4 1.3 %collective-permute-start.7 = (f32[128,128]{1,0:T(8,128)S(1)}, f32[128,128]{1,0:T(8,128)S(1)}, u32[]{:S(2)}, u32[]{:S(2)}) collective-permute-start(f32[128,128]{1,0:T(8,128)S(1)} %get-tuple-element.36.sums), channel_id=1, source_target_pairs={{0,1},{1,0},{2,3},{3,2},{4,5},{5,4},{6,7},{7,6},{8,9},{9,8},{10,11... | collective-permute-start | bytes 196616 | tf_op jit(solution)/shard_map/ppermute | solution.py:235
  30.8 4.5 %collective-permute-start.8 = (f32[128,128]{1,0:T(8,128)S(1)}, f32[128,128]{1,0:T(8,128)S(1)}, u32[]{:S(2)}, u32[]{:S(2)}) collective-permute-start(f32[128,128]{1,0:T(8,128)S(1)} %get-tuple-element.39.sums), channel_id=1, source_target_pairs={{0,1},{1,0},{2,3},{3,2},{4,5},{5,4},{6,7},{7,6},{8,9},{9,8},{10,11... | collective-permute-start | bytes 196616 | tf_op jit(solution)/shard_map/ppermute | solution.py:235

commit v2 on v1

v2 whole, which is shorter than its diff:
```python
import functools

import jax
import jax.numpy as jnp
from jax import lax
from jax.experimental import pallas as pl
from jax.experimental.pallas import tpu as pltpu
from jax.sharding import PartitionSpec as P

G = 4
LEVELS = 4
GROUPS = 2
CHUNK = 8
WAVES = ((3, 1), (0, 2))
COSTS = dict(products0=1, products1=1, inner8=1, inner32=1, scale0=1, first=1, last=1)
epsilon = 1e-06
VMEM_SCOPED = 14 * 2**20
SMEM_SPEC = pl.BlockSpec(memory_space=pltpu.SMEM)
VMEM_SPEC = pl.BlockSpec(memory_space=pltpu.VMEM)
HBM_SPEC = pl.BlockSpec(memory_space=pltpu.HBM)
ANY_SPEC = pl.BlockSpec(memory_space=pl.ANY)


def lanes():
    return lax.broadcasted_iota(jnp.int32, (128, 128), 1)


def level_of(wave, core):
    first, second = WAVES[wave]
    return jnp.where(core == 0, first, second)


def row_sums(block, weights):
    full = kept = None
    for column in range(4):
        part = jnp.abs(block[:, column * 128 : (column + 1) * 128])
        weighted = part * weights[column]
        full = part if full is None else full + part
        kept = weighted if kept is None else kept + weighted
    return jnp.sum(full, axis=1, keepdims=True), jnp.sum(kept, axis=1, keepdims=True)


def weights_of(mask, block):
    return [mask[column, block].astype(jnp.float32) for column in range(4)]


def inner_block(ids, mask, block, first, second, raw, sums):
    left = jnp.concatenate([first[k] for k in range(4)], axis=1)
    right = jnp.concatenate([second[ids[k, block]] for k in range(4)], axis=0)
    product = jnp.dot(left, right, preferred_element_type=jnp.float32)
    raw[block] = product
    full, kept = row_sums(product, weights_of(mask, block))
    lane = lanes()
    sums[...] = jnp.where(lane == block, full, jnp.where(lane == block + 64, kept, sums[...]))


def tile_copy(wave, by_level, out, sem):
    return pltpu.make_async_copy(by_level.at[level_of(wave, lax.axis_index("col"))], out, sem)


def pick_tiles(by_level, out, sem):
    copy = tile_copy(0, by_level, out, sem)
    copy.start()
    copy.wait()


def inner_head(
    count,
    tables_hbm,
    first_hbm,
    second_hbm,
    by_level,
    after,
    tables,
    raw,
    sums,
    second,
    tiles_b,
    first,
    table_sem,
    first_sem,
    second_sem,
    tile_sem,
):
    del after
    ids, mask = tables[:2]
    copies = [pltpu.make_async_copy(second_hbm, second, second_sem)]
    for place, (source, target) in enumerate(zip(tables_hbm, tables)):
        copies.append(pltpu.make_async_copy(source, target, table_sem.at[place]))
    copies.append(pltpu.make_async_copy(first_hbm.at[pl.ds(0, count)], first, first_sem))
    copies.append(tile_copy(1, by_level, tiles_b, tile_sem))
    for copy in copies:
        copy.start()
    sums[...] = jnp.zeros_like(sums)
    for copy in copies:
        copy.wait()

    @pl.loop(0, count // CHUNK)
    def _(chunk):
        for j in range(CHUNK):
            block = chunk * CHUNK + j
            inner_block(ids, mask, block, first.at[block], second, raw, sums)


def inner_rest(start, count, fresh, ids, mask, first, second, raw_in, sums_in, after, raw, sums, done):
    del raw_in, after
    done[...] = jnp.zeros_like(done)
    sums[...] = jnp.zeros_like(sums) if fresh else sums_in[...]

    @pl.loop(0, count // CHUNK)
    def _(chunk):
        for j in range(CHUNK):
            block = start + chunk * CHUNK + j
            inner_block(ids, mask, block, first.at[block], second, raw, sums)


def coupling_products(wave, send_rows, tiles, second, second_other, after, out_own, out_other):
    del after
    level = level_of(wave, lax.axis_index("col"))
    for group in range(GROUPS):
        left = jnp.concatenate([tiles[group * G + s] for s in range(G)], axis=1)
        for rows, out in ((second, out_own), (second_other, out_other)):
            right = jnp.concatenate([rows[send_rows[level, group * G + s]] for s in range(G)], axis=0)
            product = jnp.dot(left, right, preferred_element_type=jnp.float32)
            top = jnp.max(jnp.abs(product), axis=1, keepdims=True)
            power = jnp.floor(jnp.log(jnp.maximum(top, 2.0**-100)) * 1.4426950408889634) + 1.0
            scaled = jnp.round(product * jnp.exp2(15.0 - power))
            coded = jnp.clip(scaled, -32767.0, 32767.0).astype(jnp.int32).astype(jnp.int16)
            for column in range(4):
                out[pl.ds((group * 4 + column) * 128, 128), :] = coded[:, column * 128 : (column + 1) * 128]
            turned = jnp.broadcast_to(power, (128, 128)).T
            out[pl.ds(1024 + 16 * group, 16), :] = turned[:16].astype(jnp.int32).astype(jnp.int16)


def scale_part(start, mask, raw, sums, sums_other, out_in, after, out_hbm, done, out, sem):
    del out_in, after
    done[...] = jnp.zeros_like(done)
    both = sums[...] + sums_other[...]
    scale = both[:, :64] / (both[:, 64:] + epsilon)
    scale = jnp.concatenate([scale, scale], axis=1)

    def out_copy(chunk):
        span = pl.ds(chunk * CHUNK, CHUNK)
        return pltpu.make_async_copy(out.at[span], out_hbm.at[pl.ds(start + chunk * CHUNK, CHUNK)], sem.at[chunk])

    chunks = out.shape[0] // CHUNK

    @pl.loop(0, chunks)
    def _(chunk):
        for j in range(CHUNK):
            place = chunk * CHUNK + j
            block = start + place
            factor = jnp.take_along_axis(scale, jnp.full((128, 128), block, jnp.int32), axis=1)
            weights = weights_of(mask, block)
            for column in range(4):
                span = slice(column * 128, (column + 1) * 128)
                out[place, :, span] = (raw[block, :, span] * (factor * weights[column])).astype(jnp.bfloat16)
        out_copy(chunk).start()

    for chunk in range(chunks):
        out_copy(chunk).wait()


def add_part(targets, level, group, source, part, raw):
    block = targets[level * GROUPS + group]
    power = source[pl.ds(1024 + 16 * part, 16), :].astype(jnp.int32).astype(jnp.float32)
    step = jnp.exp2(jnp.concatenate([power] * 8, axis=0).T - 15.0)
    for column in range(4):
        span = slice(column * 128, (column + 1) * 128)
        coded = source[pl.ds((part * 4 + column) * 128, 128), :].astype(jnp.int32)
        raw[block, :, span] += coded.astype(jnp.float32) * step


def add_wave(wave, targets, same, cross, raw):
    core = lax.axis_index("col")
    for group in range(GROUPS):
        add_part(targets, level_of(wave, core), group, same, group, raw)
        add_part(targets, level_of(wave, 1 - core), group, cross, group, raw)


def add_first(targets, raw_in, same, cross, after, raw):
    del raw_in, after
    add_wave(0, targets, same, cross, raw)


def add_last(targets, mask, raw_in, same, cross, raw, final, sums):
    del raw_in
    add_wave(1, targets, same, cross, raw)
    lane = lanes()
    found = jnp.zeros((128, 128), jnp.float32)
    for entry in range(LEVELS * GROUPS):
        block = targets[entry]
        weights = weights_of(mask, block)
        product = raw[block]
        full, kept = row_sums(product, weights)
        found = jnp.where(lane == entry, full, jnp.where(lane == entry + 64, kept, found))
        for column in range(4):
            span = slice(column * 128, (column + 1) * 128)
            final[entry, :, span] = product[:, span] * weights[column]
    sums[...] = found


def scale_final(targets, final, sums, sums_other, out_in, out_hbm, out, sem):
    del out_in
    both = sums[...] + sums_other[...]
    scale = both[:, :64] / (both[:, 64:] + epsilon)
    blocks = [targets[entry] for entry in range(LEVELS * GROUPS)]
    latest = []
    for entry, block in enumerate(blocks):
        again = jnp.bool_(False)
        for later in blocks[entry + 1 :]:
            again = again | (later == block)
        latest.append(jnp.logical_not(again))

    def out_copy(entry):
        return pltpu.make_async_copy(out.at[entry], out_hbm.at[blocks[entry]], sem.at[entry])

    for entry in range(LEVELS * GROUPS):
        factor = jnp.broadcast_to(scale[:, entry : entry + 1], (128, 128))
        for column in range(4):
            span = slice(column * 128, (column + 1) * 128)
            out[entry, :, span] = (final[entry, :, span] * factor).astype(jnp.bfloat16)
        pl.when(latest[entry])(lambda entry=entry: out_copy(entry).start())
    for entry in range(LEVELS * GROUPS):
        pl.when(latest[entry])(lambda entry=entry: out_copy(entry).wait())


def call(kernel, name, outs, in_specs, out_specs, scratch=(), aliases=None, flops=1):
    return pl.pallas_call(
        kernel,
        out_shape=outs,
        in_specs=in_specs,
        out_specs=out_specs,
        scratch_shapes=list(scratch),
        input_output_aliases=aliases or {},
        compiler_params=pltpu.CompilerParams(vmem_limit_bytes=VMEM_SCOPED),
        cost_estimate=pl.CostEstimate(flops=flops, bytes_accessed=1, transcendentals=0),
        name=name,
    )


def route(count, wave, swap):
    pairs = []
    for domain in range(count):
        for core in range(2):
            other = domain ^ (1 << WAVES[wave][core])
            pairs.append((domain * 2 + core, other * 2 + (core ^ swap)))
    return pairs


def in_hbm(array):
    return pltpu.with_memory_space_constraint(array, pltpu.HBM)


def in_vmem(array):
    return pltpu.with_memory_space_constraint(array, pltpu.VMEM)


def swap_cores(block):
    return lax.ppermute(block, "col", [(0, 1), (1, 0)])


def on_device(first_interp, first_ids, second_interp, coupling, send_rows, targets, keep_mask):
    fine = first_interp.shape[0]
    cuts = 8, 32
    count = lax.axis_size("dom")
    token = pltpu.VMEM((8, 128), jnp.float32)
    raw_shape = pltpu.VMEM((fine, 128, 512), jnp.float32)
    sums_shape = pltpu.VMEM((128, 128), jnp.float32)

    by_level = in_hbm(coupling.reshape(LEVELS, 8, 128, 128))
    tile_shape = pltpu.VMEM((8, 128, 128), jnp.bfloat16)
    tiles_a = call(pick_tiles, "pick_tiles", tile_shape, [HBM_SPEC], VMEM_SPEC, [pltpu.SemaphoreType.DMA])(by_level)
    second_other = swap_cores(second_interp)

    first = in_vmem(first_interp)
    tables = [in_hbm(x) for x in (first_ids.T, keep_mask.T, send_rows, targets)]
    head = cuts[0]
    tables, raw, sums, second, tiles_b = call(
        functools.partial(inner_head, head),
        "inner_head",
        (
            [pltpu.SMEM(x.shape, x.dtype) for x in tables],
            raw_shape,
            sums_shape,
            pltpu.VMEM((8, 128, 512), jnp.bfloat16),
            tile_shape,
        ),
        [[HBM_SPEC] * 4, HBM_SPEC, HBM_SPEC, HBM_SPEC, VMEM_SPEC],
        ([SMEM_SPEC] * 4,) + (VMEM_SPEC,) * 4,
        [
            pltpu.VMEM((head, 4, 128, 128), jnp.bfloat16),
            pltpu.SemaphoreType.DMA((4,)),
            pltpu.SemaphoreType.DMA,
            pltpu.SemaphoreType.DMA,
            pltpu.SemaphoreType.DMA,
        ],
    )(tables, in_hbm(first_interp), in_hbm(second_interp), by_level, tiles_a)
    came = [
        lax.ppermute(own, ("dom", "col"), route(count, wave, 0)) for wave, own in enumerate((tiles_a, tiles_b))
    ]
    ids, mask, send_rows, targets = tables

    def inner_part(start, stop, raw, sums, after, fresh=False):
        return call(
            functools.partial(inner_rest, start, stop - start, fresh),
            "inner_rest",
            (raw_shape, sums_shape, token),
            [SMEM_SPEC, SMEM_SPEC, VMEM_SPEC, VMEM_SPEC, VMEM_SPEC, VMEM_SPEC, VMEM_SPEC],
            (VMEM_SPEC,) * 3,
            aliases={4: 0} if fresh else {4: 0, 5: 1},
            flops=COSTS[f"inner{start}"],
        )(ids, mask, first, second, raw, sums, after)

    def products(wave, after):
        outs = call(
            functools.partial(coupling_products, wave),
            "coupling_products",
            (pltpu.VMEM((1056, 128), jnp.int16),) * 2,
            [SMEM_SPEC, VMEM_SPEC, VMEM_SPEC, VMEM_SPEC, VMEM_SPEC],
            (VMEM_SPEC,) * 2,
            flops=COSTS[f"products{wave}"],
        )(send_rows, came[wave], second, second_other, after)
        return outs, [lax.ppermute(x, ("dom", "col"), route(count, wave, swap)) for swap, x in enumerate(outs)]

    def scaled(start, stop, sums, out, after):
        return call(
            functools.partial(scale_part, start),
            "scale_part",
            (jax.ShapeDtypeStruct((fine, 128, 512), jnp.bfloat16), token),
            [SMEM_SPEC, VMEM_SPEC, VMEM_SPEC, VMEM_SPEC, HBM_SPEC if start else VMEM_SPEC, VMEM_SPEC],
            (HBM_SPEC, VMEM_SPEC),
            [pltpu.VMEM((stop - start, 128, 512), jnp.bfloat16), pltpu.SemaphoreType.DMA(((stop - start) // CHUNK,))],
            aliases={4: 0} if start else None,
            flops=COSTS[f"scale{start}"],
        )(mask, raw, sums, swap_cores(sums), out, after)

    raw, sums, done = inner_part(cuts[0], cuts[1], raw, sums, second)
    outs, (same_a, cross_a) = products(0, done)
    outs, (same_b, cross_b) = products(1, outs[0])
    raw, sums, done = inner_part(cuts[1], fine, raw, sums, outs[0])
    out, done = scaled(0, fine, sums, done, done)
    raw = call(
        add_first,
        "add_first",
        raw_shape,
        [SMEM_SPEC] + [VMEM_SPEC] * 4,
        VMEM_SPEC,
        aliases={1: 0},
        flops=COSTS["first"],
    )(targets, raw, same_a, cross_a, done)
    _, final, sums = call(
        add_last,
        "add_last",
        (raw_shape, pltpu.VMEM((8, 128, 512), jnp.float32), sums_shape),
        [SMEM_SPEC, SMEM_SPEC] + [VMEM_SPEC] * 3,
        (VMEM_SPEC,) * 3,
        aliases={2: 0},
        flops=COSTS["last"],
    )(targets, mask, raw, same_b, cross_b)
    return call(
        scale_final,
        "scale_final",
        jax.ShapeDtypeStruct((fine, 128, 512), jnp.bfloat16),
        [SMEM_SPEC, VMEM_SPEC, VMEM_SPEC, VMEM_SPEC, HBM_SPEC],
        HBM_SPEC,
        [pltpu.VMEM((8, 128, 512), jnp.bfloat16), pltpu.SemaphoreType.DMA((8,))],
        aliases={4: 0},
    )(targets, final, sums, swap_cores(sums), out)


def solution(mesh):
    return jax.shard_map(
        on_device,
        mesh=mesh,
        in_specs=(
            P("dom", None, None, None),
            P("dom", None),
            P("dom", None, "col"),
            P("dom", None, None),
            P("dom", None),
            P("dom"),
            P("dom", "col"),
        ),
        out_specs=P("dom", None, "col"),
        check_vma=False,
    )
```

time: 36.5 us -> 33.4 us (0.915)
  waiting for transfers between devices: 3.82 us -> 2.14 us
  Pallas kernels: 17.6 us -> 16.4 us
    pallas_call x1, Pallas kernels: 4.39 us -> 2.46 us  [on_device(): call(functools.partial(inner_head, head), 'inner_head', ([pltpu.SMEM(x.sh...]
    ppermute x6, waiting for transfers between devices: 1.67 us -> 0.33 us  [the longest x4 0.32 us: products(): lax.ppermute(x, ('dom', 'col'), route(count, wave, swap))]
    ppermute x3, starting transfers between devices: 6.9 us -> 6.13 us  [swap_cores(): return lax.ppermute(block, 'col', [(0, 1), (1, 0)])]
    pallas_call x5 -> x6, Pallas kernels: 10.7 us -> 11.5 us  [the longest x2 5.73 us: inner_part(): call(functools.partial(inner_rest, start, stop - start, fresh), 'inner_re...]
    ppermute x6, starting transfers between devices: 8.04 us -> 8.5 us  [the longest x4 5.23 us: products(): lax.ppermute(x, ('dom', 'col'), route(count, wave, swap))]
  transfers between devices with their start and end apart: 9 -> 9, of which waited for: 4 -> 3; matrix products, arithmetic and copies ran while one was open for 0% -> 0% of each run, Pallas kernels for 41% -> 43%
where the time goes in v2:
time: 33.4 us; the launch traced here: 33.3 us
  Pallas kernels  16.4 us (49%)
  starting transfers between devices  14.6 us (44%)
  waiting for transfers between devices  2.14 us (6%)
    ppermute x3, starting transfers between devices, swap_cores(): return lax.ppermute(block, 'col', [(0, 1), (1, 0)])  6.13 us
    pallas_call x2, Pallas kernels, inner_part(): call(functools.partial(inner_rest, start, stop - start, fresh), 'inner_re...  5.73 us
    ppermute x4, starting transfers between devices, products(): lax.ppermute(x, ('dom', 'col'), route(count, wave, swap))  5.23 us
    pallas_call x1, Pallas kernels, scaled(): call(functools.partial(scale_part, start), 'scale_part', (jax.ShapeDtypeS...  3.83 us
    ppermute x2, starting transfers between devices, on_device(): lax.ppermute(own, ('dom', 'col'), route(count, wave, 0))  3.27 us
    pallas_call x1, Pallas kernels, on_device(): call(functools.partial(inner_head, head), 'inner_head', ([pltpu.SMEM(x.sh...  2.46 us
    ppermute x3, waiting for transfers between devices, swap_cores(): return lax.ppermute(block, 'col', [(0, 1), (1, 0)])  1.81 us
    pallas_call x2, Pallas kernels, products(): call(functools.partial(coupling_products, wave), 'coupling_products', (pl...  1.24 us
  transfers between devices with their start and end apart: 9, of which 3 were waited for; matrix products, arithmetic and copies ran while one was open for 0% of the time, Pallas kernels for 43%

profile of v2, /device:TPU:1, one launch (start us, length us, event | category | flops | bytes accessed | tf_op | source)
XLA Modules:
  0.0 33.3 jit_solution(11607525969886708542)
XLA Ops:
  0.0 0.0 copy-start
  0.0 3.2 %collective-permute-start.1 = (bf16[8,128,512]{2,1,0:T(8,128)(2,1)}, bf16[8,128,512]{2,1,0:T(8,128)(2,1)S(1)}, u32[]{:S(2)}, u32[]{:S(2)}) collective-permute-start(bf16[8,128,512]{2,1,0:T(8,128)(2,1)} %second_hbm.1), channel_id=1, source_target_pairs={{0,1},{1,0},{2,3},{3,2},{4,5},{5,4},{6,7},{7,6},{8,9},{9,8},{10,11... | collective-permute-start | bytes 3145736 | tf_op jit(solution)/shard_map/ppermute | solution.py:260
  3.2 1.0 %pick_tiles.1.after = bf16[8,128,128]{2,1,0:T(8,128)(2,1)S(1)} custom-call(bf16[4,8,128,128]{3,2,1,0:T(8,128)(2,1)} %bitcast.3), custom_call_target="tpu_custom_call" | custom-call | flops 1 | bytes 1 | tf_op jit(solution)/shard_map/pick_tiles/pallas_call | solution.py:273
  4.2 1.5 %collective-permute-start.2 = (bf16[8,128,128]{2,1,0:T(8,128)(2,1)S(1)}, bf16[8,128,128]{2,1,0:T(8,128)(2,1)S(1)}, u32[]{:S(2)}, u32[]{:S(2)}) collective-permute-start(bf16[8,128,128]{2,1,0:T(8,128)(2,1)S(1)} %pick_tiles.1.after), channel_id=1, source_target_pairs={{0,16},{1,5},{2,18},{3,7},{4,20},{5,1},{6,22},{7,3},{8,24},{9,13},... | collective-permute-start | bytes 786440 | tf_op jit(solution)/shard_map/ppermute | solution.py:300
  5.8 2.5 %inner_head.1 = (s32[4,64]{1,0:T(4,128)S(4)}, s32[4,64]{1,0:T(4,128)S(4)}, s32[4,8]{1,0:T(4,128)S(4)}, s32[8]{0:T(128)S(4)}, f32[64,128,512]{2,1,0:T(8,128)S(1)}...) custom-call(s32[4,64]{1,0:T(4,128)} %bitcast.5, s32[4,64]{1,0:T(4,128)} %bitcast.6, ...), custom_call_target="tpu_custom_call" | custom-call | flops 1 | bytes 1 | tf_op jit(solution)/shard_map/inner_head/pallas_call | solution.py:279
  8.2 1.7 %collective-permute-start = (bf16[8,128,128]{2,1,0:T(8,128)(2,1)S(1)}, bf16[8,128,128]{2,1,0:T(8,128)(2,1)S(1)}, u32[]{:S(2)}, u32[]{:S(2)}) collective-permute-start(bf16[8,128,128]{2,1,0:T(8,128)(2,1)S(1)} %get-tuple-element.36), channel_id=1, source_target_pairs={{0,2},{1,9},{2,0},{3,11},{4,6},{5,13},{6,4},{7,15},{8,10},{9,1},{1... | collective-permute-start | bytes 786440 | tf_op jit(solution)/shard_map/ppermute | solution.py:300
  9.9 0.0 copy-done
  9.9 2.5 %inner_rest.2 = (f32[64,128,512]{2,1,0:T(8,128)S(1)}, f32[128,128]{1,0:T(8,128)S(1)}, f32[8,128]{1,0:T(8,128)S(1)}) custom-call(s32[4,64]{1,0:T(4,128)S(4)} %get-tuple-element.29.ids, s32[4,64]{1,0:T(4,128)S(4)} %get-tuple-element.28.mask, bf16[64,4,128,128]{3,2,1,0:T(8,128)(2,1)S(1)} %copy-done, ...), custom_call_target="tpu_custom_call", output_to_operand_aliasing={{0}: (4, {}), {1}: (5, {})} | custom-call | flops 1 | bytes 1 | tf_op jit(solution)/shard_map/inner_rest/pallas_call | solution.py:305
  12.4 0.0 collective-permute-done.2.tiles
  12.4 0.0 collective-permute-done.1.second_other
  12.4 0.6 %coupling_products.2 = (s16[1056,128]{1,0:T(8,128)(2,1)S(1)}, s16[1056,128]{1,0:T(8,128)(2,1)S(1)}) custom-call(s32[4,8]{1,0:T(4,128)S(4)} %get-tuple-element.35.send_rows, bf16[8,128,128]{2,1,0:T(8,128)(2,1)S(1)} %collective-permute-done.2.tiles, bf16[8,128,512]{2,1,0:T(8,128)(2,1)S(1)} %get-tuple-element.30.second.after, ...), custom_call_target="tpu_custom_call" | custom-call | flops 1 | bytes 1 | tf_op jit(solution)/shard_map/coupling_products/pallas_call | solution.py:316
  13.0 3.7 %collective-permute-start.4 = (s16[1056,128]{1,0:T(8,128)(2,1)S(1)}, s16[1056,128]{1,0:T(8,128)(2,1)S(1)}, u32[]{:S(2)}, u32[]{:S(2)}) collective-permute-start(s16[1056,128]{1,0:T(8,128)(2,1)S(1)} %get-tuple-element.41), channel_id=1, source_target_pairs={{0,17},{1,4},{2,19},{3,6},{4,21},{5,0},{6,23},{7,2},{8,25},{9,12},... | collective-permute-start | bytes 811016 | tf_op jit(solution)/shard_map/ppermute | solution.py:324
  16.7 1.4 %collective-permute-start.3 = (s16[1056,128]{1,0:T(8,128)(2,1)S(1)}, s16[1056,128]{1,0:T(8,128)(2,1)S(1)}, u32[]{:S(2)}, u32[]{:S(2)}) collective-permute-start(s16[1056,128]{1,0:T(8,128)(2,1)S(1)} %get-tuple-element.38.after), channel_id=1, source_target_pairs={{0,16},{1,5},{2,18},{3,7},{4,20},{5,1},{6,22},{7,3},{8,24},{9,13},... | collective-permute-start | bytes 811016 | tf_op jit(solution)/shard_map/ppermute | solution.py:324
  18.1 0.0 collective-permute-done.tiles
  18.1 0.6 %coupling_products.3 = (s16[1056,128]{1,0:T(8,128)(2,1)S(1)}, s16[1056,128]{1,0:T(8,128)(2,1)S(1)}) custom-call(s32[4,8]{1,0:T(4,128)S(4)} %get-tuple-element.35.send_rows, bf16[8,128,128]{2,1,0:T(8,128)(2,1)S(1)} %collective-permute-done.tiles, bf16[8,128,512]{2,1,0:T(8,128)(2,1)S(1)} %get-tuple-element.30.second.after, ...), custom_call_target="tpu_custom_call" | custom-call | flops 1 | bytes 1 | tf_op jit(solution)/shard_map/coupling_products/pallas_call | solution.py:316
  18.8 0.1 collective-permute-start.7
  18.8 0.1 collective-permute-start.6
  18.9 3.3 %inner_rest.3 = (f32[64,128,512]{2,1,0:T(8,128)S(1)}, f32[128,128]{1,0:T(8,128)S(1)}, f32[8,128]{1,0:T(8,128)S(1)}) custom-call(s32[4,64]{1,0:T(4,128)S(4)} %get-tuple-element.29.ids, s32[4,64]{1,0:T(4,128)S(4)} %get-tuple-element.28.mask, bf16[64,4,128,128]{3,2,1,0:T(8,128)(2,1)S(1)} %copy-done, ...), custom_call_target="tpu_custom_call", output_to_operand_aliasing={{0}: (4, {}), {1}: (5, {})} | custom-call | flops 1 | bytes 1 | tf_op jit(solution)/shard_map/inner_rest/pallas_call | solution.py:305
  22.2 2.1 %collective-permute-start.5 = (f32[128,128]{1,0:T(8,128)S(1)}, f32[128,128]{1,0:T(8,128)S(1)}, u32[]{:S(2)}, u32[]{:S(2)}) collective-permute-start(f32[128,128]{1,0:T(8,128)S(1)} %get-tuple-element.42.sums), channel_id=1, source_target_pairs={{0,1},{1,0},{2,3},{3,2},{4,5},{5,4},{6,7},{7,6},{8,9},{9,8},{10,11... | collective-permute-start | bytes 196616 | tf_op jit(solution)/shard_map/ppermute | solution.py:260
  24.3 0.9 %collective-permute-done.5.sums_other = f32[128,128]{1,0:T(8,128)S(1)} collective-permute-done((f32[128,128]{1,0:T(8,128)S(1)}, f32[128,128]{1,0:T(8,128)S(1)}, u32[]{:S(2)}, u32[]{:S(2)}) %collective-permute-start.5) | collective-permute-done | bytes 65568 | tf_op jit(solution)/shard_map/ppermute | solution.py:260
  25.2 3.8 %scale_part.1 = (bf16[64,128,512]{2,1,0:T(8,128)(2,1)}, f32[8,128]{1,0:T(8,128)S(1)}) custom-call(s32[4,64]{1,0:T(4,128)S(4)} %get-tuple-element.28.mask, f32[64,128,512]{2,1,0:T(8,128)S(1)} %get-tuple-element.40.raw.raw_in, f32[128,128]{1,0:T(8,128)S(1)} %get-tuple-element.42.sums, f32[128,128]{1,0:T(8,128)S(1)} %collective-permute-done.5.sums_other, ...), custom_call_target="tpu_custom_call" | custom-call | flops 1 | bytes 1 | tf_op jit(solution)/shard_map/scale_part/pallas_call | solution.py:327
  29.1 0.0 collective-permute-done.4.cross
  29.1 0.0 collective-permute-done.3.same
  29.1 0.2 add_first.1.raw_in
  29.3 0.0 collective-permute-done.7.cross
  29.3 0.3 collective-permute-done.6.same
  29.7 0.7 %add_last.1 = (f32[64,128,512]{2,1,0:T(8,128)S(1)}, f32[8,128,512]{2,1,0:T(8,128)S(1)}, f32[128,128]{1,0:T(8,128)S(1)}) custom-call(s32[8]{0:T(128)S(4)} %get-tuple-element.27.targets, s32[4,64]{1,0:T(4,128)S(4)} %get-tuple-element.28.mask, f32[64,128,512]{2,1,0:T(8,128)S(1)} %add_first.1.raw_in, ...), custom_call_target="tpu_custom_call", output_to_operand_aliasing={{0}: (2, {})} | custom-call | flops 1 | bytes 1 | tf_op jit(solution)/shard_map/add_last/pallas_call | solution.py:352
  30.4 0.8 %collective-permute-start.8 = (f32[128,128]{1,0:T(8,128)S(1)}, f32[128,128]{1,0:T(8,128)S(1)}, u32[]{:S(2)}, u32[]{:S(2)}) collective-permute-start(f32[128,128]{1,0:T(8,128)S(1)} %get-tuple-element.47.sums), channel_id=1, source_target_pairs={{0,1},{1,0},{2,3},{3,2},{4,5},{5,4},{6,7},{7,6},{8,9},{9,8},{10,11... | collective-permute-start | bytes 196616 | tf_op jit(solution)/shard_map/ppermute | solution.py:260
  31.2 0.9 %collective-permute-done.8.sums_other = f32[128,128]{1,0:T(8,128)S(1)} collective-permute-done((f32[128,128]{1,0:T(8,128)S(1)}, f32[128,128]{1,0:T(8,128)S(1)}, u32[]{:S(2)}, u32[]{:S(2)}) %collective-permute-start.8) | collective-permute-done | bytes 65568 | tf_op jit(solution)/shard_map/ppermute | solution.py:260
  32.1 1.2 %scale_final.1 = bf16[64,128,512]{2,1,0:T(8,128)(2,1)} custom-call(s32[8]{0:T(128)S(4)} %get-tuple-element.27.targets, f32[8,128,512]{2,1,0:T(8,128)S(1)} %get-tuple-element.46.final, f32[128,128]{1,0:T(8,128)S(1)} %get-tuple-element.47.sums, f32[128,128]{1,0:T(8,128)S(1)} %collective-permute-done.8.sums_other, ...), custom_call_target="tpu_custom_call", output_to_operand_aliasing={{}: (4, {})} | custom-call | flops 1 | bytes 1 | tf_op jit(solution)/shard_map/scale_final/pallas_call | solution.py:361
Async XLA Ops:
  0.0 9.9 %copy-start = (bf16[64,4,128,128]{3,2,1,0:T(8,128)(2,1)S(1)}, bf16[64,4,128,128]{3,2,1,0:T(8,128)(2,1)}, u32[]{:S(2)}) copy-start(bf16[64,4,128,128]{3,2,1,0:T(8,128)(2,1)} %first.3) | copy-start | bytes 25165828
  0.0 12.4 %collective-permute-start.1 = (bf16[8,128,512]{2,1,0:T(8,128)(2,1)}, bf16[8,128,512]{2,1,0:T(8,128)(2,1)S(1)}, u32[]{:S(2)}, u32[]{:S(2)}) collective-permute-start(bf16[8,128,512]{2,1,0:T(8,128)(2,1)} %second_hbm.1), channel_id=1, source_target_pairs={{0,1},{1,0},{2,3},{3,2},{4,5},{5,4},{6,7},{7,6},{8,9},{9,8},{10,11... | collective-permute-start | bytes 3145736 | tf_op jit(solution)/shard_map/ppermute | solution.py:260
  4.2 8.2 %collective-permute-start.2 = (bf16[8,128,128]{2,1,0:T(8,128)(2,1)S(1)}, bf16[8,128,128]{2,1,0:T(8,128)(2,1)S(1)}, u32[]{:S(2)}, u32[]{:S(2)}) collective-permute-start(bf16[8,128,128]{2,1,0:T(8,128)(2,1)S(1)} %pick_tiles.1.after), channel_id=1, source_target_pairs={{0,16},{1,5},{2,18},{3,7},{4,20},{5,1},{6,22},{7,3},{8,24},{9,13},... | collective-permute-start | bytes 786440 | tf_op jit(solution)/shard_map/ppermute | solution.py:300
  8.2 9.9 %collective-permute-start = (bf16[8,128,128]{2,1,0:T(8,128)(2,1)S(1)}, bf16[8,128,128]{2,1,0:T(8,128)(2,1)S(1)}, u32[]{:S(2)}, u32[]{:S(2)}) collective-permute-start(bf16[8,128,128]{2,1,0:T(8,128)(2,1)S(1)} %get-tuple-element.36), channel_id=1, source_target_pairs={{0,2},{1,9},{2,0},{3,11},{4,6},{5,13},{6,4},{7,15},{8,10},{9,1},{1... | collective-permute-start | bytes 786440 | tf_op jit(solution)/shard_map/ppermute | solution.py:300
  13.0 16.0 %collective-permute-start.4 = (s16[1056,128]{1,0:T(8,128)(2,1)S(1)}, s16[1056,128]{1,0:T(8,128)(2,1)S(1)}, u32[]{:S(2)}, u32[]{:S(2)}) collective-permute-start(s16[1056,128]{1,0:T(8,128)(2,1)S(1)} %get-tuple-element.41), channel_id=1, source_target_pairs={{0,17},{1,4},{2,19},{3,6},{4,21},{5,0},{6,23},{7,2},{8,25},{9,12},... | collective-permute-start | bytes 811016 | tf_op jit(solution)/shard_map/ppermute | solution.py:324
  16.7 12.4 %collective-permute-start.3 = (s16[1056,128]{1,0:T(8,128)(2,1)S(1)}, s16[1056,128]{1,0:T(8,128)(2,1)S(1)}, u32[]{:S(2)}, u32[]{:S(2)}) collective-permute-start(s16[1056,128]{1,0:T(8,128)(2,1)S(1)} %get-tuple-element.38.after), channel_id=1, source_target_pairs={{0,16},{1,5},{2,18},{3,7},{4,20},{5,1},{6,22},{7,3},{8,24},{9,13},... | collective-permute-start | bytes 811016 | tf_op jit(solution)/shard_map/ppermute | solution.py:324
  18.8 10.6 %collective-permute-start.7 = (s16[1056,128]{1,0:T(8,128)(2,1)S(1)}, s16[1056,128]{1,0:T(8,128)(2,1)S(1)}, u32[]{:S(2)}, u32[]{:S(2)}) collective-permute-start(s16[1056,128]{1,0:T(8,128)(2,1)S(1)} %get-tuple-element.45), channel_id=1, source_target_pairs={{0,3},{1,8},{2,1},{3,10},{4,7},{5,12},{6,5},{7,14},{8,11},{9,0},{1... | collective-permute-start | bytes 811016 | tf_op jit(solution)/shard_map/ppermute | solution.py:324
  18.8 10.8 %collective-permute-start.6 = (s16[1056,128]{1,0:T(8,128)(2,1)S(1)}, s16[1056,128]{1,0:T(8,128)(2,1)S(1)}, u32[]{:S(2)}, u32[]{:S(2)}) collective-permute-start(s16[1056,128]{1,0:T(8,128)(2,1)S(1)} %get-tuple-element.39.after), channel_id=1, source_target_pairs={{0,2},{1,9},{2,0},{3,11},{4,6},{5,13},{6,4},{7,15},{8,10},{9,1},{1... | collective-permute-start | bytes 811016 | tf_op jit(solution)/shard_map/ppermute | solution.py:324
  22.2 3.0 %collective-permute-start.5 = (f32[128,128]{1,0:T(8,128)S(1)}, f32[128,128]{1,0:T(8,128)S(1)}, u32[]{:S(2)}, u32[]{:S(2)}) collective-permute-start(f32[128,128]{1,0:T(8,128)S(1)} %get-tuple-element.42.sums), channel_id=1, source_target_pairs={{0,1},{1,0},{2,3},{3,2},{4,5},{5,4},{6,7},{7,6},{8,9},{9,8},{10,11... | collective-permute-start | bytes 196616 | tf_op jit(solution)/shard_map/ppermute | solution.py:260
  30.4 1.7 %collective-permute-start.8 = (f32[128,128]{1,0:T(8,128)S(1)}, f32[128,128]{1,0:T(8,128)S(1)}, u32[]{:S(2)}, u32[]{:S(2)}) collective-permute-start(f32[128,128]{1,0:T(8,128)S(1)} %get-tuple-element.47.sums), channel_id=1, source_target_pairs={{0,1},{1,0},{2,3},{3,2},{4,5},{5,4},{6,7},{7,6},{8,9},{9,8},{10,11... | collective-permute-start | bytes 196616 | tf_op jit(solution)/shard_map/ppermute | solution.py:260

commit v3 on v2

--- a/solution.py
+++ b/solution.py
@@ -132,12 +132,16 @@
             out[pl.ds(1024 + 16 * group, 16), :] = turned[:16].astype(jnp.int32).astype(jnp.int16)
 
 
+def scale_of(sums, sums_other):
+    both = sums[...] + sums_other[...]
+    scale = both[:, :64] / (both[:, 64:] + epsilon)
+    return jnp.concatenate([scale, scale], axis=1)
+
+
 def scale_part(start, mask, raw, sums, sums_other, out_in, after, out_hbm, done, out, sem):
     del out_in, after
     done[...] = jnp.zeros_like(done)
-    both = sums[...] + sums_other[...]
-    scale = both[:, :64] / (both[:, 64:] + epsilon)
-    scale = jnp.concatenate([scale, scale], axis=1)
+    scale = scale_of(sums, sums_other)
 
     def out_copy(chunk):
         span = pl.ds(chunk * CHUNK, CHUNK)
@@ -171,58 +175,60 @@
         raw[block, :, span] += coded.astype(jnp.float32) * step
 
 
-def add_wave(wave, targets, same, cross, raw):
+def entries(wave):
+    return [level * GROUPS + group for level in sorted(WAVES[wave]) for group in range(GROUPS)]
+
+
+ORDER = entries(0) + entries(1)
+
+
+def add_wave(wave, targets, mask, same, cross, raw, found):
     core = lax.axis_index("col")
     for group in range(GROUPS):
         add_part(targets, level_of(wave, core), group, same, group, raw)
         add_part(targets, level_of(wave, 1 - core), group, cross, group, raw)
-
-
-def add_first(targets, raw_in, same, cross, after, raw):
+    lane = lanes()
+    for entry in entries(wave):
+        block = targets[entry]
+        full, kept = row_sums(raw[block], weights_of(mask, block))
+        place = ORDER.index(entry)
+        found = jnp.where(lane == place, full, jnp.where(lane == place + 64, kept, found))
+    return found
+
+
+def add_first(targets, mask, raw_in, same, cross, after, raw, sums):
     del raw_in, after
-    add_wave(0, targets, same, cross, raw)
-
-
-def add_last(targets, mask, raw_in, same, cross, raw, final, sums):
+    sums[...] = add_wave(0, targets, mask, same, cross, raw, jnp.zeros((128, 128), jnp.float32))
+
+
+def add_last(targets, mask, raw_in, same, cross, sums_in, raw, sums):
     del raw_in
-    add_wave(1, targets, same, cross, raw)
-    lane = lanes()
-    found = jnp.zeros((128, 128), jnp.float32)
-    for entry in range(LEVELS * GROUPS):
-        block = targets[entry]
+    sums[...] = add_wave(1, targets, mask, same, cross, raw, sums_in[...])
+
+
+def scale_final(targets, mask, raw, sums, sums_other, out_in, out_hbm, out, sem):
+    del out_in
+    scale = scale_of(sums, sums_other)
+    blocks = [targets[entry] for entry in ORDER]
+    latest = []
+    for place, block in enumerate(blocks):
+        again = jnp.bool_(False)
+        for later in blocks[place + 1 :]:
+            again = again | (later == block)
+        latest.append(jnp.logical_not(again))
+
+    def out_copy(place):
+        return pltpu.make_async_copy(out.at[place], out_hbm.at[blocks[place]], sem.at[place])
+
+    for place, block in enumerate(blocks):
+        factor = jnp.broadcast_to(scale[:, place : place + 1], (128, 128))
         weights = weights_of(mask, block)
-        product = raw[block]
-        full, kept = row_sums(product, weights)
-        found = jnp.where(lane == entry, full, jnp.where(lane == entry + 64, kept, found))
         for column in range(4):
             span = slice(column * 128, (column + 1) * 128)
-            final[entry, :, span] = product[:, span] * weights[column]
-    sums[...] = found
-
-
-def scale_final(targets, final, sums, sums_other, out_in, out_hbm, out, sem):
-    del out_in
-    both = sums[...] + sums_other[...]
-    scale = both[:, :64] / (both[:, 64:] + epsilon)
-    blocks = [targets[entry] for entry in range(LEVELS * GROUPS)]
-    latest = []
-    for entry, block in enumerate(blocks):
-        again = jnp.bool_(False)
-        for later in blocks[entry + 1 :]:
-            again = again | (later == block)
-        latest.append(jnp.logical_not(again))
-
-    def out_copy(entry):
-        return pltpu.make_async_copy(out.at[entry], out_hbm.at[blocks[entry]], sem.at[entry])
-
-    for entry in range(LEVELS * GROUPS):
-        factor = jnp.broadcast_to(scale[:, entry : entry + 1], (128, 128))
-        for column in range(4):
-            span = slice(column * 128, (column + 1) * 128)
-            out[entry, :, span] = (final[entry, :, span] * factor).astype(jnp.bfloat16)
-        pl.when(latest[entry])(lambda entry=entry: out_copy(entry).start())
-    for entry in range(LEVELS * GROUPS):
-        pl.when(latest[entry])(lambda entry=entry: out_copy(entry).wait())
+            out[place, :, span] = (raw[block, :, span] * (factor * weights[column])).astype(jnp.bfloat16)
+        pl.when(latest[place])(lambda place=place: out_copy(place).start())
+    for place in range(len(blocks)):
+        pl.when(latest[place])(lambda place=place: out_copy(place).wait())
 
 
 def call(kernel, name, outs, in_specs, out_specs, scratch=(), aliases=None, flops=1):
@@ -340,33 +346,33 @@
     outs, (same_b, cross_b) = products(1, outs[0])
     raw, sums, done = inner_part(cuts[1], fine, raw, sums, outs[0])
     out, done = scaled(0, fine, sums, done, done)
-    raw = call(
+    raw, sums = call(
         add_first,
         "add_first",
-        raw_shape,
-        [SMEM_SPEC] + [VMEM_SPEC] * 4,
-        VMEM_SPEC,
-        aliases={1: 0},
+        (raw_shape, sums_shape),
+        [SMEM_SPEC, SMEM_SPEC] + [VMEM_SPEC] * 4,
+        (VMEM_SPEC,) * 2,
+        aliases={2: 0},
         flops=COSTS["first"],
-    )(targets, raw, same_a, cross_a, done)
-    _, final, sums = call(
+    )(targets, mask, raw, same_a, cross_a, done)
+    raw, sums = call(
         add_last,
         "add_last",
-        (raw_shape, pltpu.VMEM((8, 128, 512), jnp.float32), sums_shape),
-        [SMEM_SPEC, SMEM_SPEC] + [VMEM_SPEC] * 3,
-        (VMEM_SPEC,) * 3,
-        aliases={2: 0},
+        (raw_shape, sums_shape),
+        [SMEM_SPEC, SMEM_SPEC] + [VMEM_SPEC] * 4,
+        (VMEM_SPEC,) * 2,
+        aliases={2: 0, 5: 1},
         flops=COSTS["last"],
-    )(targets, mask, raw, same_b, cross_b)
+    )(targets, mask, raw, same_b, cross_b, sums)
     return call(
         scale_final,
         "scale_final",
         jax.ShapeDtypeStruct((fine, 128, 512), jnp.bfloat16),
-        [SMEM_SPEC, VMEM_SPEC, VMEM_SPEC, VMEM_SPEC, HBM_SPEC],
+        [SMEM_SPEC, SMEM_SPEC, VMEM_SPEC, VMEM_SPEC, VMEM_SPEC, HBM_SPEC],
         HBM_SPEC,
         [pltpu.VMEM((8, 128, 512), jnp.bfloat16), pltpu.SemaphoreType.DMA((8,))],
-        aliases={4: 0},
-    )(targets, final, sums, swap_cores(sums), out)
+        aliases={5: 0},
+    )(targets, mask, raw, sums, swap_cores(sums), out)
 
 
 def solution(mesh):

time: 33.4 us -> 33.2 us (level)
  transfers between devices with their start and end apart: 9 -> 9, of which waited for: 3 -> 3; matrix products, arithmetic and copies ran while one was open for 0% -> 0% of each run, Pallas kernels for 43% -> 44%
where the time goes in v3:
time: 33.2 us; the launch traced here: 33.1 us
  Pallas kernels  16.4 us (49%)
  starting transfers between devices  14.6 us (44%)
  waiting for transfers between devices  1.9 us (6%)
    ppermute x3, starting transfers between devices, swap_cores(): return lax.ppermute(block, 'col', [(0, 1), (1, 0)])  6.13 us
    pallas_call x2, Pallas kernels, inner_part(): call(functools.partial(inner_rest, start, stop - start, fresh), 'inner_re...  5.73 us
    ppermute x4, starting transfers between devices, products(): lax.ppermute(x, ('dom', 'col'), route(count, wave, swap))  5.23 us
    pallas_call x1, Pallas kernels, scaled(): call(functools.partial(scale_part, start), 'scale_part', (jax.ShapeDtypeS...  3.83 us
    ppermute x2, starting transfers between devices, on_device(): lax.ppermute(own, ('dom', 'col'), route(count, wave, 0))  3.27 us
    pallas_call x1, Pallas kernels, on_device(): call(functools.partial(inner_head, head), 'inner_head', ([pltpu.SMEM(x.sh...  2.46 us
    ppermute x3, waiting for transfers between devices, swap_cores(): return lax.ppermute(block, 'col', [(0, 1), (1, 0)])  1.81 us
    pallas_call x1, Pallas kernels, on_device(): call(scale_final, 'scale_final', jax.ShapeDtypeStruct((fine, 128, 512), j...  1.27 us
  transfers between devices with their start and end apart: 9, of which 3 were waited for; matrix products, arithmetic and copies ran while one was open for 0% of the time, Pallas kernels for 44%

profile of v3, /device:TPU:1, one launch (start us, length us, event | category | flops | bytes accessed | tf_op | source)
XLA Modules:
  0.0 33.1 jit_solution(13553060157615318262)
XLA Ops:
  0.0 0.0 copy-start
  0.0 3.2 %collective-permute-start.1 = (bf16[8,128,512]{2,1,0:T(8,128)(2,1)}, bf16[8,128,512]{2,1,0:T(8,128)(2,1)S(1)}, u32[]{:S(2)}, u32[]{:S(2)}) collective-permute-start(bf16[8,128,512]{2,1,0:T(8,128)(2,1)} %second_hbm.1), channel_id=1, source_target_pairs={{0,1},{1,0},{2,3},{3,2},{4,5},{5,4},{6,7},{7,6},{8,9},{9,8},{10,11... | collective-permute-start | bytes 3145736 | tf_op jit(solution)/shard_map/ppermute | solution.py:266
  3.2 1.0 %pick_tiles.1.after = bf16[8,128,128]{2,1,0:T(8,128)(2,1)S(1)} custom-call(bf16[4,8,128,128]{3,2,1,0:T(8,128)(2,1)} %bitcast.3), custom_call_target="tpu_custom_call" | custom-call | flops 1 | bytes 1 | tf_op jit(solution)/shard_map/pick_tiles/pallas_call | solution.py:279
  4.2 1.5 %collective-permute-start.2 = (bf16[8,128,128]{2,1,0:T(8,128)(2,1)S(1)}, bf16[8,128,128]{2,1,0:T(8,128)(2,1)S(1)}, u32[]{:S(2)}, u32[]{:S(2)}) collective-permute-start(bf16[8,128,128]{2,1,0:T(8,128)(2,1)S(1)} %pick_tiles.1.after), channel_id=1, source_target_pairs={{0,16},{1,5},{2,18},{3,7},{4,20},{5,1},{6,22},{7,3},{8,24},{9,13},... | collective-permute-start | bytes 786440 | tf_op jit(solution)/shard_map/ppermute | solution.py:306
  5.8 2.5 %inner_head.1 = (s32[4,64]{1,0:T(4,128)S(4)}, s32[4,64]{1,0:T(4,128)S(4)}, s32[4,8]{1,0:T(4,128)S(4)}, s32[8]{0:T(128)S(4)}, f32[64,128,512]{2,1,0:T(8,128)S(1)}...) custom-call(s32[4,64]{1,0:T(4,128)} %bitcast.5, s32[4,64]{1,0:T(4,128)} %bitcast.6, ...), custom_call_target="tpu_custom_call" | custom-call | flops 1 | bytes 1 | tf_op jit(solution)/shard_map/inner_head/pallas_call | solution.py:285
  8.2 1.7 %collective-permute-start = (bf16[8,128,128]{2,1,0:T(8,128)(2,1)S(1)}, bf16[8,128,128]{2,1,0:T(8,128)(2,1)S(1)}, u32[]{:S(2)}, u32[]{:S(2)}) collective-permute-start(bf16[8,128,128]{2,1,0:T(8,128)(2,1)S(1)} %get-tuple-element.38), channel_id=1, source_target_pairs={{0,2},{1,9},{2,0},{3,11},{4,6},{5,13},{6,4},{7,15},{8,10},{9,1},{1... | collective-permute-start | bytes 786440 | tf_op jit(solution)/shard_map/ppermute | solution.py:306
  9.9 0.0 copy-done
  9.9 2.5 %inner_rest.2 = (f32[64,128,512]{2,1,0:T(8,128)S(1)}, f32[128,128]{1,0:T(8,128)S(1)}, f32[8,128]{1,0:T(8,128)S(1)}) custom-call(s32[4,64]{1,0:T(4,128)S(4)} %get-tuple-element.31.ids, s32[4,64]{1,0:T(4,128)S(4)} %get-tuple-element.30.mask, bf16[64,4,128,128]{3,2,1,0:T(8,128)(2,1)S(1)} %copy-done, ...), custom_call_target="tpu_custom_call", output_to_operand_aliasing={{0}: (4, {}), {1}: (5, {})} | custom-call | flops 1 | bytes 1 | tf_op jit(solution)/shard_map/inner_rest/pallas_call | solution.py:311
  12.4 0.0 collective-permute-done.2.tiles
  12.4 0.0 collective-permute-done.1.second_other
  12.4 0.6 %coupling_products.2 = (s16[1056,128]{1,0:T(8,128)(2,1)S(1)}, s16[1056,128]{1,0:T(8,128)(2,1)S(1)}) custom-call(s32[4,8]{1,0:T(4,128)S(4)} %get-tuple-element.37.send_rows, bf16[8,128,128]{2,1,0:T(8,128)(2,1)S(1)} %collective-permute-done.2.tiles, bf16[8,128,512]{2,1,0:T(8,128)(2,1)S(1)} %get-tuple-element.32.second.after, ...), custom_call_target="tpu_custom_call" | custom-call | flops 1 | bytes 1 | tf_op jit(solution)/shard_map/coupling_products/pallas_call | solution.py:322
  13.0 3.7 %collective-permute-start.4 = (s16[1056,128]{1,0:T(8,128)(2,1)S(1)}, s16[1056,128]{1,0:T(8,128)(2,1)S(1)}, u32[]{:S(2)}, u32[]{:S(2)}) collective-permute-start(s16[1056,128]{1,0:T(8,128)(2,1)S(1)} %get-tuple-element.43), channel_id=1, source_target_pairs={{0,17},{1,4},{2,19},{3,6},{4,21},{5,0},{6,23},{7,2},{8,25},{9,12},... | collective-permute-start | bytes 811016 | tf_op jit(solution)/shard_map/ppermute | solution.py:330
  16.7 1.4 %collective-permute-start.3 = (s16[1056,128]{1,0:T(8,128)(2,1)S(1)}, s16[1056,128]{1,0:T(8,128)(2,1)S(1)}, u32[]{:S(2)}, u32[]{:S(2)}) collective-permute-start(s16[1056,128]{1,0:T(8,128)(2,1)S(1)} %get-tuple-element.40.after), channel_id=1, source_target_pairs={{0,16},{1,5},{2,18},{3,7},{4,20},{5,1},{6,22},{7,3},{8,24},{9,13},... | collective-permute-start | bytes 811016 | tf_op jit(solution)/shard_map/ppermute | solution.py:330
  18.1 0.0 collective-permute-done.tiles
  18.1 0.6 %coupling_products.3 = (s16[1056,128]{1,0:T(8,128)(2,1)S(1)}, s16[1056,128]{1,0:T(8,128)(2,1)S(1)}) custom-call(s32[4,8]{1,0:T(4,128)S(4)} %get-tuple-element.37.send_rows, bf16[8,128,128]{2,1,0:T(8,128)(2,1)S(1)} %collective-permute-done.tiles, bf16[8,128,512]{2,1,0:T(8,128)(2,1)S(1)} %get-tuple-element.32.second.after, ...), custom_call_target="tpu_custom_call" | custom-call | flops 1 | bytes 1 | tf_op jit(solution)/shard_map/coupling_products/pallas_call | solution.py:322
  18.8 0.1 collective-permute-start.7
  18.8 0.1 collective-permute-start.6
  18.9 3.3 %inner_rest.3 = (f32[64,128,512]{2,1,0:T(8,128)S(1)}, f32[128,128]{1,0:T(8,128)S(1)}, f32[8,128]{1,0:T(8,128)S(1)}) custom-call(s32[4,64]{1,0:T(4,128)S(4)} %get-tuple-element.31.ids, s32[4,64]{1,0:T(4,128)S(4)} %get-tuple-element.30.mask, bf16[64,4,128,128]{3,2,1,0:T(8,128)(2,1)S(1)} %copy-done, ...), custom_call_target="tpu_custom_call", output_to_operand_aliasing={{0}: (4, {}), {1}: (5, {})} | custom-call | flops 1 | bytes 1 | tf_op jit(solution)/shard_map/inner_rest/pallas_call | solution.py:311
  22.2 2.1 %collective-permute-start.5 = (f32[128,128]{1,0:T(8,128)S(1)}, f32[128,128]{1,0:T(8,128)S(1)}, u32[]{:S(2)}, u32[]{:S(2)}) collective-permute-start(f32[128,128]{1,0:T(8,128)S(1)} %get-tuple-element.44.sums), channel_id=1, source_target_pairs={{0,1},{1,0},{2,3},{3,2},{4,5},{5,4},{6,7},{7,6},{8,9},{9,8},{10,11... | collective-permute-start | bytes 196616 | tf_op jit(solution)/shard_map/ppermute | solution.py:266
  24.3 0.9 %collective-permute-done.5.sums_other = f32[128,128]{1,0:T(8,128)S(1)} collective-permute-done((f32[128,128]{1,0:T(8,128)S(1)}, f32[128,128]{1,0:T(8,128)S(1)}, u32[]{:S(2)}, u32[]{:S(2)}) %collective-permute-start.5) | collective-permute-done | bytes 65568 | tf_op jit(solution)/shard_map/ppermute | solution.py:266
  25.2 3.8 %scale_part.1 = (bf16[64,128,512]{2,1,0:T(8,128)(2,1)}, f32[8,128]{1,0:T(8,128)S(1)}) custom-call(s32[4,64]{1,0:T(4,128)S(4)} %get-tuple-element.30.mask, f32[64,128,512]{2,1,0:T(8,128)S(1)} %get-tuple-element.42.raw.raw_in, f32[128,128]{1,0:T(8,128)S(1)} %get-tuple-element.44.sums, f32[128,128]{1,0:T(8,128)S(1)} %collective-permute-done.5.sums_other, ...), custom_call_target="tpu_custom_call" | custom-call | flops 1 | bytes 1 | tf_op jit(solution)/shard_map/scale_part/pallas_call | solution.py:333
  29.1 0.0 collective-permute-done.4.cross
  29.1 0.0 collective-permute-done.3.same
  29.1 0.5 %add_first.1 = (f32[64,128,512]{2,1,0:T(8,128)S(1)}, f32[128,128]{1,0:T(8,128)S(1)}) custom-call(s32[8]{0:T(128)S(4)} %get-tuple-element.29.targets, s32[4,64]{1,0:T(4,128)S(4)} %get-tuple-element.30.mask, f32[64,128,512]{2,1,0:T(8,128)S(1)} %get-tuple-element.42.raw.raw_in, ...), custom_call_target="tpu_custom_call", output_to_operand_aliasing={{0}: (2, {})} | custom-call | flops 1 | bytes 1 | tf_op jit(solution)/shard_map/add_first/pallas_call | solution.py:349
  29.6 0.0 collective-permute-done.7.cross
  29.6 0.1 collective-permute-done.6.same
  29.7 0.5 %add_last.1 = (f32[64,128,512]{2,1,0:T(8,128)S(1)}, f32[128,128]{1,0:T(8,128)S(1)}) custom-call(s32[8]{0:T(128)S(4)} %get-tuple-element.29.targets, s32[4,64]{1,0:T(4,128)S(4)} %get-tuple-element.30.mask, f32[64,128,512]{2,1,0:T(8,128)S(1)} %get-tuple-element.47.raw_in, ...), custom_call_target="tpu_custom_call", output_to_operand_aliasing={{0}: (2, {}), {1}: (5, {})} | custom-call | flops 1 | bytes 1 | tf_op jit(solution)/shard_map/add_last/pallas_call | solution.py:358
  30.1 0.8 %collective-permute-start.8 = (f32[128,128]{1,0:T(8,128)S(1)}, f32[128,128]{1,0:T(8,128)S(1)}, u32[]{:S(2)}, u32[]{:S(2)}) collective-permute-start(f32[128,128]{1,0:T(8,128)S(1)} %get-tuple-element.51.sums), channel_id=1, source_target_pairs={{0,1},{1,0},{2,3},{3,2},{4,5},{5,4},{6,7},{7,6},{8,9},{9,8},{10,11... | collective-permute-start | bytes 196616 | tf_op jit(solution)/shard_map/ppermute | solution.py:266
  30.9 0.9 %collective-permute-done.8.sums_other = f32[128,128]{1,0:T(8,128)S(1)} collective-permute-done((f32[128,128]{1,0:T(8,128)S(1)}, f32[128,128]{1,0:T(8,128)S(1)}, u32[]{:S(2)}, u32[]{:S(2)}) %collective-permute-start.8) | collective-permute-done | bytes 65568 | tf_op jit(solution)/shard_map/ppermute | solution.py:266
  31.8 1.3 %scale_final.1 = bf16[64,128,512]{2,1,0:T(8,128)(2,1)} custom-call(s32[8]{0:T(128)S(4)} %get-tuple-element.29.targets, s32[4,64]{1,0:T(4,128)S(4)} %get-tuple-element.30.mask, f32[64,128,512]{2,1,0:T(8,128)S(1)} %get-tuple-element.50.raw, f32[128,128]{1,0:T(8,128)S(1)} %get-tuple-element.51.sums, ...), custom_call_target="tpu_custom_call", output_to_operand_aliasing={{}: (5, {})} | custom-call | flops 1 | bytes 1 | tf_op jit(solution)/shard_map/scale_final/pallas_call | solution.py:367
Async XLA Ops:
  0.0 9.9 %copy-start = (bf16[64,4,128,128]{3,2,1,0:T(8,128)(2,1)S(1)}, bf16[64,4,128,128]{3,2,1,0:T(8,128)(2,1)}, u32[]{:S(2)}) copy-start(bf16[64,4,128,128]{3,2,1,0:T(8,128)(2,1)} %first.3) | copy-start | bytes 25165828
  0.0 12.4 %collective-permute-start.1 = (bf16[8,128,512]{2,1,0:T(8,128)(2,1)}, bf16[8,128,512]{2,1,0:T(8,128)(2,1)S(1)}, u32[]{:S(2)}, u32[]{:S(2)}) collective-permute-start(bf16[8,128,512]{2,1,0:T(8,128)(2,1)} %second_hbm.1), channel_id=1, source_target_pairs={{0,1},{1,0},{2,3},{3,2},{4,5},{5,4},{6,7},{7,6},{8,9},{9,8},{10,11... | collective-permute-start | bytes 3145736 | tf_op jit(solution)/shard_map/ppermute | solution.py:266
  4.2 8.2 %collective-permute-start.2 = (bf16[8,128,128]{2,1,0:T(8,128)(2,1)S(1)}, bf16[8,128,128]{2,1,0:T(8,128)(2,1)S(1)}, u32[]{:S(2)}, u32[]{:S(2)}) collective-permute-start(bf16[8,128,128]{2,1,0:T(8,128)(2,1)S(1)} %pick_tiles.1.after), channel_id=1, source_target_pairs={{0,16},{1,5},{2,18},{3,7},{4,20},{5,1},{6,22},{7,3},{8,24},{9,13},... | collective-permute-start | bytes 786440 | tf_op jit(solution)/shard_map/ppermute | solution.py:306
  8.2 9.9 %collective-permute-start = (bf16[8,128,128]{2,1,0:T(8,128)(2,1)S(1)}, bf16[8,128,128]{2,1,0:T(8,128)(2,1)S(1)}, u32[]{:S(2)}, u32[]{:S(2)}) collective-permute-start(bf16[8,128,128]{2,1,0:T(8,128)(2,1)S(1)} %get-tuple-element.38), channel_id=1, source_target_pairs={{0,2},{1,9},{2,0},{3,11},{4,6},{5,13},{6,4},{7,15},{8,10},{9,1},{1... | collective-permute-start | bytes 786440 | tf_op jit(solution)/shard_map/ppermute | solution.py:306
  13.0 16.0 %collective-permute-start.4 = (s16[1056,128]{1,0:T(8,128)(2,1)S(1)}, s16[1056,128]{1,0:T(8,128)(2,1)S(1)}, u32[]{:S(2)}, u32[]{:S(2)}) collective-permute-start(s16[1056,128]{1,0:T(8,128)(2,1)S(1)} %get-tuple-element.43), channel_id=1, source_target_pairs={{0,17},{1,4},{2,19},{3,6},{4,21},{5,0},{6,23},{7,2},{8,25},{9,12},... | collective-permute-start | bytes 811016 | tf_op jit(solution)/shard_map/ppermute | solution.py:330
  16.7 12.4 %collective-permute-start.3 = (s16[1056,128]{1,0:T(8,128)(2,1)S(1)}, s16[1056,128]{1,0:T(8,128)(2,1)S(1)}, u32[]{:S(2)}, u32[]{:S(2)}) collective-permute-start(s16[1056,128]{1,0:T(8,128)(2,1)S(1)} %get-tuple-element.40.after), channel_id=1, source_target_pairs={{0,16},{1,5},{2,18},{3,7},{4,20},{5,1},{6,22},{7,3},{8,24},{9,13},... | collective-permute-start | bytes 811016 | tf_op jit(solution)/shard_map/ppermute | solution.py:330
  18.8 10.8 %collective-permute-start.7 = (s16[1056,128]{1,0:T(8,128)(2,1)S(1)}, s16[1056,128]{1,0:T(8,128)(2,1)S(1)}, u32[]{:S(2)}, u32[]{:S(2)}) collective-permute-start(s16[1056,128]{1,0:T(8,128)(2,1)S(1)} %get-tuple-element.48), channel_id=1, source_target_pairs={{0,3},{1,8},{2,1},{3,10},{4,7},{5,12},{6,5},{7,14},{8,11},{9,0},{1... | collective-permute-start | bytes 811016 | tf_op jit(solution)/shard_map/ppermute | solution.py:330
  18.8 10.8 %collective-permute-start.6 = (s16[1056,128]{1,0:T(8,128)(2,1)S(1)}, s16[1056,128]{1,0:T(8,128)(2,1)S(1)}, u32[]{:S(2)}, u32[]{:S(2)}) collective-permute-start(s16[1056,128]{1,0:T(8,128)(2,1)S(1)} %get-tuple-element.41.after), channel_id=1, source_target_pairs={{0,2},{1,9},{2,0},{3,11},{4,6},{5,13},{6,4},{7,15},{8,10},{9,1},{1... | collective-permute-start | bytes 811016 | tf_op jit(solution)/shard_map/ppermute | solution.py:330
  22.2 3.0 %collective-permute-start.5 = (f32[128,128]{1,0:T(8,128)S(1)}, f32[128,128]{1,0:T(8,128)S(1)}, u32[]{:S(2)}, u32[]{:S(2)}) collective-permute-start(f32[128,128]{1,0:T(8,128)S(1)} %get-tuple-element.44.sums), channel_id=1, source_target_pairs={{0,1},{1,0},{2,3},{3,2},{4,5},{5,4},{6,7},{7,6},{8,9},{9,8},{10,11... | collective-permute-start | bytes 196616 | tf_op jit(solution)/shard_map/ppermute | solution.py:266
  30.1 1.7 %collective-permute-start.8 = (f32[128,128]{1,0:T(8,128)S(1)}, f32[128,128]{1,0:T(8,128)S(1)}, u32[]{:S(2)}, u32[]{:S(2)}) collective-permute-start(f32[128,128]{1,0:T(8,128)S(1)} %get-tuple-element.51.sums), channel_id=1, source_target_pairs={{0,1},{1,0},{2,3},{3,2},{4,5},{5,4},{6,7},{7,6},{8,9},{9,8},{10,11... | collective-permute-start | bytes 196616 | tf_op jit(solution)/shard_map/ppermute | solution.py:266
